TPU v7x, 128 devices: a whole 4x4x4 slice. The times are simulated.
128 devices in a mesh: tile: 8 (over x, core), tm: 4 (over y), plane: 4 (over z).
Axes of the slice: x: 4, y: 4, z: 4, core: 2. Of those that a mesh axis runs over, the one named last changes fastest.
Arguments:
- movie: bfloat16 [8192, 128, 512], P(('tile', 'plane'), None, 'tm'), may hold values from -6 to 6
- footprint: bfloat16 [32768, 128], P(('tile', 'plane')), may hold values from 0 to 0.5
- entry_block: int32 [32768], P(('tile', 'plane')), may hold values from 0 to 255
- entry_owner: int32 [32768, 1], P(('tile', 'plane')), may hold values from 0 to 31; in each aligned block of 1024 rows (0 to 1023, 1024 to 2047, ...) at most 96 rows name the same one
- entry_slot: int32 [32768], P(('tile', 'plane')), may hold values from 0 to 255
- traces: float32 [8192, 512], P(('tile', 'plane'), 'tm'), may hold values from -6 to 6
- slow_root: float32 [8192], P(('tile', 'plane')), may hold values from 0.9 to 0.995
- fast_root: float32 [8192], P(('tile', 'plane')), may hold values from 0.2 to 0.7
Outputs:
- reconstruction: bfloat16 [8192, 128, 512], P(('tile', 'plane'), None, 'tm')
- calcium: float32 [8192, 512], P(('tile', 'plane'), 'tm')
Inputs may be any that keep to these rules, and one draw needn't show every extreme that they name: `entry_owner`: among the 1024 footprint blocks of one device, at most 96 name one owner, a bound that some block reaches.
All inputs are finite; a program needn't handle non-finite values.
Results may differ from a plain program's by a relative error of at most 0.0038.
Values sent between devices are 32-bit elements; how exact they have to be, the bound alone decides.
A program may use at most 128 MiB of HBM per device.

v0:
```python
import jax
import jax.numpy as jnp
from jax import lax
from jax.sharding import PartitionSpec as P

SWEEPS = 4


HIGH = lax.Precision.HIGHEST


def shifted(value, axis, steps):
    count = lax.axis_size(axis)
    leading, last = (max(0, -steps), min(count, count - steps))
    return lax.ppermute(value, axis, [(source, source + steps) for source in range(leading, last)])


def prefix_2(value, axis, join, neutral):
    count, mine = (lax.axis_size(axis), lax.axis_index(axis))
    pieces = jax.tree.map(lambda part: lax.all_gather(part, axis), value)
    total = jax.tree.map(
        lambda part, zero: jnp.full_like(part, 0) + jnp.asarray(zero, part.dtype), value, neutral
    )

    def step(position, total):
        longer = join(total, jax.tree.map(lambda part: part[position], pieces))
        return jax.tree.map(lambda new, old: jnp.where(position < mine, new, old), longer, total)

    return lax.fori_loop(0, count - 1, step, total)


def compose(earlier, subsequent):
    return (
        subsequent[0] * earlier[0] + subsequent[1] * earlier[2],
        subsequent[0] * earlier[1] + subsequent[1] * earlier[3],
        subsequent[2] * earlier[0] + subsequent[3] * earlier[2],
        subsequent[2] * earlier[1] + subsequent[3] * earlier[3],
        subsequent[0] * earlier[4] + subsequent[1] * earlier[5] + subsequent[4],
        subsequent[2] * earlier[4] + subsequent[3] * earlier[5] + subsequent[5],
    )


def shards(movie, footprint, entry_block, entry_owner, entry_slot, traces, slow_root, fast_root):
    owners = lax.axis_size(("tile", "plane"))
    entries = footprint.shape[0]
    neurons_own = traces.shape[0]
    frames = traces.shape[1]
    gathered = jnp.take(movie, entry_block, axis=0)
    projected = jnp.einsum("ev,evf->ef", footprint, gathered, preferred_element_type=jnp.float32)
    foot_values = footprint.astype(jnp.float32)
    energy_terms = jnp.sum(foot_values * foot_values, axis=1)
    owner_ids = entry_owner[:, 0]
    neuron = owner_ids * neurons_own + entry_slot
    member = (neuron[:, None] == jnp.arange(owners * neurons_own, dtype=jnp.int32)[None, :]).astype(
        jnp.float32
    )
    partial_rows = jnp.dot(member.T, projected, precision=HIGH)
    partial_energy = jnp.dot(member.T, energy_terms, precision=HIGH)
    summed, energy = (
        lax.psum_scatter(partial_rows, ("tile", "plane"), scatter_dimension=0, tiled=True),
        lax.psum_scatter(partial_energy, ("tile", "plane"), scatter_dimension=0, tiled=True),
    )
    target = (summed + traces) / (energy[:, None] + 1.0)
    lag_one = slow_root + fast_root
    lag_two = -slow_root * fast_root
    ones_grid = jnp.ones_like(target)
    zeros_grid = jnp.zeros_like(target)
    estimate = target
    for sweep_index in range(SWEEPS):
        previous = shifted(estimate[:, -2:], "tm", 1)
        extended = jnp.concatenate([previous, estimate], axis=1)
        spikes = jnp.maximum(
            estimate - lag_one[:, None] * extended[:, 1:-1] - lag_two[:, None] * extended[:, :-2],
            0.0,
        )
        elements = (
            lag_one[:, None] * ones_grid,
            lag_two[:, None] * ones_grid,
            ones_grid,
            zeros_grid,
            spikes,
            zeros_grid,
        )
        prefix = lax.associative_scan(compose, elements, axis=1)
        block_map = tuple((member_arr[:, -1] for member_arr in prefix))
        ones_vec = jnp.ones_like(lag_one)
        zeros_vec = jnp.zeros_like(lag_one)
        entering = prefix_2(
            block_map,
            "tm",
            compose,
            (ones_vec, zeros_vec, zeros_vec, ones_vec, zeros_vec, zeros_vec),
        )
        calcium = prefix[4] + prefix[0] * entering[4][:, None] + prefix[1] * entering[5][:, None]
        if sweep_index + 1 < SWEEPS:
            estimate = 0.5 * (target + calcium)
    every_trace = lax.all_gather(calcium, ("tile", "plane"), axis=0, tiled=True)
    entry_rows = jnp.dot(member, every_trace, precision=HIGH)
    rows_rounded = entry_rows.astype(jnp.bfloat16)
    n_blocks = movie.shape[0]
    n_vox = movie.shape[1]
    group_size = 8
    block_hot = (jnp.arange(n_blocks, dtype=jnp.int32)[:, None] == entry_block[None, :]).astype(
        jnp.bfloat16
    )
    foot_groups = footprint.T.reshape(n_vox // group_size, group_size, entries)

    def voxel_group(foot_part):
        weighted = block_hot[:, None, :] * foot_part[None, :, :]
        return jnp.einsum("bge,et->bgt", weighted, rows_rounded, preferred_element_type=jnp.float32)

    grouped = lax.map(voxel_group, foot_groups)
    rebuilt = jnp.transpose(grouped, (1, 0, 2, 3)).reshape(n_blocks, n_vox, frames)
    return (rebuilt.astype(jnp.bfloat16), calcium)


def solution(mesh):
    placed = (
        P(("tile", "plane"), None, "tm"),
        P(("tile", "plane"), None),
        P(("tile", "plane")),
        P(("tile", "plane"), None),
        P(("tile", "plane")),
        P(("tile", "plane"), "tm"),
        P(("tile", "plane")),
        P(("tile", "plane")),
    )
    return jax.shard_map(
        shards,
        mesh=mesh,
        in_specs=placed,
        out_specs=(P(("tile", "plane"), None, "tm"), P(("tile", "plane"), "tm")),
        check_vma=False,
    )
```

profile of v0, /device:TPU:0, one launch (start us, length us, event | category | flops | bytes accessed | tf_op | source)
XLA Modules:
  0.0 457.4 jit_solution(14900289009662048246)
XLA Ops:
  10.0 24.4 %gather_fusion = bf16[1024,128,128]{2,1,0:T(8,128)(2,1)} fusion(bf16[256,128,128]{2,1,0:T(8,128)(2,1)} %param.18, s32[1024]{0:T(1024)S(1)} %fusion.50), kind=kCustom, calls=%fused_computation | custom fusion | bytes 67112960 | tf_op jit(solution)/shard_map/jit(_take)/gather | solution.py:48
  34.3 14.1 %fusion.14 = f32[1024,1,128]{2,1,0:T(1,128)S(1)} fusion(bf16[1024,128,128]{2,1,0:T(8,128)(2,1)} %gather_fusion, pred[1024]{0:T(1024)(128)(4,1)S(1)} %compare_and_fusion, bf16[1024,128,1]{1,0,2:T(8,128)(2,1)S(1)} %bitcast.147), kind=kOutput, calls=%fused_computation.53 | convolution fusion | flops 50331648 | bytes 34341888 | tf_op jit(solution)/shard_map/ev,evf->ef/dot_general | solution.py:49
  48.5 13.3 %fusion.17 = f32[8192,128]{0,1:T(8,128)} fusion(f32[1024,128]{1,0:T(8,128)S(1)} %bitcast.255, s32[1024]{0:T(1024)S(1)} %add.1881), kind=kOutput, calls=%fused_computation.57 | convolution fusion | flops 12893290496 | bytes 4722688 | tf_op jit(solution)/shard_map/dot_general | solution.py:57
  62.8 10.2 %all-gather.4 = f32[1024,1]{0,1:T(1,128)S(1)} all-gather(f32[256,1]{0,1:T(1,128)S(1)} %slice.3177), channel_id=6, replica_groups=mesh['tile'=8,'tm'=4,'plane'=4] {'tm'}, dimensions={0}, use_global_device_ids=true | all-gather | bytes 5120 | tf_op jit(solution)/shard_map/all_gather | solution.py:20
  76.4 14.6 %fusion.19 = f32[1,8192]{1,0:T(1,128)S(1)} fusion(f32[1024,1]{0,1:T(1,128)S(1)} %bitcast.254, s32[1024]{0:T(1024)S(1)} %add.1881), kind=kOutput, calls=%fused_computation.59 | convolution fusion | flops 109051904 | bytes 40960 | tf_op jit(solution)/shard_map/dot_general | solution.py:58
  91.1 128.0 %all-reduce.174 = f32[8192]{0:T(1024)S(1)} all-reduce(f32[8192]{0:T(1024)S(1)} %bitcast.244), channel_id=15, replica_groups=mesh['tile'=8,'tm'=4,'plane'=4] {'tile','plane'}, use_global_device_ids=true, to_apply=%region_2.3.clone | all-reduce | flops 8192 | bytes 65536
  221.5 8.3 %all-gather.3 = f32[1024,1]{0,1:T(1,128)S(1)} all-gather(f32[256,1]{0,1:T(1,128)S(1)} %slice.3175), channel_id=5, replica_groups=mesh['tile'=8,'tm'=4,'plane'=4] {'tm'}, dimensions={0}, use_global_device_ids=true | all-gather | bytes 5120 | tf_op jit(solution)/shard_map/all_gather | solution.py:20
  232.0 7.7 %all-gather.5 = f32[1024,1]{0,1:T(1,128)S(1)} all-gather(f32[256,1]{0,1:T(1,128)S(1)} %slice.3179), channel_id=7, replica_groups=mesh['tile'=8,'tm'=4,'plane'=4] {'tm'}, dimensions={0}, use_global_device_ids=true | all-gather | bytes 5120 | tf_op jit(solution)/shard_map/all_gather | solution.py:20
  240.5 8.3 %all-gather.2 = f32[1024,1]{0,1:T(1,128)S(1)} all-gather(f32[256,1]{0,1:T(1,128)S(1)} %slice_add_fusion.75), channel_id=4, replica_groups=mesh['tile'=8,'tm'=4,'plane'=4] {'tm'}, dimensions={0}, use_global_device_ids=true | all-gather | bytes 5120 | tf_op jit(solution)/shard_map/all_gather | solution.py:20
  249.4 7.7 %all-gather.1 = f32[1024,1]{0,1:T(1,128)S(1)} all-gather(f32[256,1]{0,1:T(1,128)S(1)} %slice_add_fusion.76), channel_id=3, replica_groups=mesh['tile'=8,'tm'=4,'plane'=4] {'tm'}, dimensions={0}, use_global_device_ids=true | all-gather | bytes 5120 | tf_op jit(solution)/shard_map/all_gather | solution.py:20
  257.7 8.3 %all-gather = f32[1024,1]{0,1:T(1,128)S(1)} all-gather(f32[256,1]{0,1:T(1,128)S(1)} %slice_add_fusion.77), channel_id=2, replica_groups=mesh['tile'=8,'tm'=4,'plane'=4] {'tm'}, dimensions={0}, use_global_device_ids=true | all-gather | bytes 5120 | tf_op jit(solution)/shard_map/all_gather | solution.py:20
  267.0 2.6 collective-permute-start.1
  272.5 9.2 %all-gather.7 = f32[1024,1]{0,1:T(1,128)S(1)} all-gather(f32[256,1]{0,1:T(1,128)S(1)} %slice.3181), channel_id=9, replica_groups=mesh['tile'=8,'tm'=4,'plane'=4] {'tm'}, dimensions={0}, use_global_device_ids=true | all-gather | bytes 5120 | tf_op jit(solution)/shard_map/all_gather | solution.py:20
  282.5 7.0 %all-gather.6 = f32[1024,1]{0,1:T(1,128)S(1)} all-gather(f32[256,1]{0,1:T(1,128)S(1)} %slice_add_fusion.70), channel_id=8, replica_groups=mesh['tile'=8,'tm'=4,'plane'=4] {'tm'}, dimensions={0}, use_global_device_ids=true | all-gather | bytes 5120 | tf_op jit(solution)/shard_map/all_gather | solution.py:20
  290.4 3.9 collective-permute-start.2
  297.3 9.2 %all-gather.9 = f32[1024,1]{0,1:T(1,128)S(1)} all-gather(f32[256,1]{0,1:T(1,128)S(1)} %slice.3183), channel_id=11, replica_groups=mesh['tile'=8,'tm'=4,'plane'=4] {'tm'}, dimensions={0}, use_global_device_ids=true | all-gather | bytes 5120 | tf_op jit(solution)/shard_map/all_gather | solution.py:20
  307.3 7.0 %all-gather.8 = f32[1024,1]{0,1:T(1,128)S(1)} all-gather(f32[256,1]{0,1:T(1,128)S(1)} %slice_add_fusion.65), channel_id=10, replica_groups=mesh['tile'=8,'tm'=4,'plane'=4] {'tm'}, dimensions={0}, use_global_device_ids=true | all-gather | bytes 5120 | tf_op jit(solution)/shard_map/all_gather | solution.py:20
  315.2 3.9 collective-permute-start.3
  322.0 9.2 %all-gather.11 = f32[1024,1]{0,1:T(1,128)S(1)} all-gather(f32[256,1]{0,1:T(1,128)S(1)} %slice.3185), channel_id=13, replica_groups=mesh['tile'=8,'tm'=4,'plane'=4] {'tm'}, dimensions={0}, use_global_device_ids=true | all-gather | bytes 5120 | tf_op jit(solution)/shard_map/all_gather | solution.py:20
  332.0 7.0 %all-gather.10 = f32[1024,1]{0,1:T(1,128)S(1)} all-gather(f32[256,1]{0,1:T(1,128)S(1)} %slice_add_fusion.60), channel_id=12, replica_groups=mesh['tile'=8,'tm'=4,'plane'=4] {'tm'}, dimensions={0}, use_global_device_ids=true | all-gather | bytes 5120 | tf_op jit(solution)/shard_map/all_gather | solution.py:20
  342.8 43.0 %all-gather.14.cloned.1.call-done = f32[8192,128]{0,1:T(8,128)} async-done(((f32[256,128]{0,1:T(8,128)}), f32[8192,128]{0,1:T(8,128)}) %all-gather.14.cloned.1.call-update) | async-done | bytes 4194320 | tf_op jit(solution)/shard_map/all_gather | solution.py:97
  385.8 17.3 %fusion.24 = bf16[1024,128]{1,0:T(8,128)(2,1)S(1)} fusion(f32[8192,128]{0,1:T(8,128)} %all-gather.14.cloned.1.call-done, s32[1024]{0:T(1024)S(1)} %add.1881), kind=kOutput, calls=%fused_computation.66 | convolution fusion | flops 12893421568 | bytes 4460544 | tf_op jit(solution)/shard_map/dot_general | solution.py:98
  403.1 35.1 %while.75 = (s32[]{:T(128)}, bf16[16,256,8,128]{3,1,2,0:T(8,128)(2,1)}, bf16[16,8,1024]{2,1,0:T(8,128)(2,1)S(1)}, bf16[1024,128]{1,0:T(8,128)(2,1)S(1)}, s32[1024]{0:T(1024)S(1)}, /*index=5*/s32[]{:T(128)}) while((s32[]{:T(128)}, bf16[16,256,8,128]{3,1,2,0:T(8,128)(2,1)}, bf16[16,8,1024]{2,1,0:T(8,128)(2,1)S(1)}, ...), condition=%wide.region_12.13_spmd.clone, body=%wide.region_11.12_spmd.clone.sunk | while | flops 539492352 | bytes 2413129 | solution.py:112
  405.5 2.1 fusion.78
  407.7 2.1 fusion.78
  418.6 2.1 fusion.78
  422.9 2.1 fusion.78
  425.1 2.1 fusion.78
  431.7 2.1 fusion.78
  433.9 2.1 fusion.78
  436.1 2.1 fusion.78
  438.2 12.2 %copy.555 = bf16[256,16,8,128]{3,2,1,0:T(8,128)(2,1)} copy(bf16[256,16,8,128]{3,0,2,1:T(8,128)(2,1)} %bitcast.145) | data formatting | bytes 16777216 | tf_op jit(solution)/shard_map/convert_element_type | solution.py:114
  (685 shorter events, 46.8 us)
Async XLA Ops:
  7.2 211.9 %reduce-scatter.2.cloned.1.call-start = ((), (), s32[]{:S(2)}) async-start(), calls=%async_computation.1 | async-start | bytes 4325376 | tf_op jit(solution)/shard_map/reduce_scatter | solution.py:60
  10.0 24.4 %copy-start = (bf16[1024,128]{1,0:T(8,128)(2,1)S(1)}, bf16[1024,128]{1,0:T(8,128)(2,1)}, u32[]{:S(2)}) copy-start(bf16[1024,128]{1,0:T(8,128)(2,1)} %param.19) | copy-start | bytes 786436
  48.5 13.4 %copy-start.2 = (f32[256,128]{1,0:T(8,128)S(1)}, f32[256,128]{1,0:T(8,128)}, u32[]{:S(2)}) copy-start(f32[256,128]{1,0:T(8,128)} %param.23) | copy-start | bytes 393220
  48.5 13.5 %copy-start.3 = (f32[256]{0:T(256)S(1)}, f32[256]{0:T(256)}, u32[]{:S(2)}) copy-start(f32[256]{0:T(256)} %param.25) | copy-start | bytes 3076
  48.5 13.5 %copy-start.4 = (f32[256]{0:T(256)S(1)}, f32[256]{0:T(256)}, u32[]{:S(2)}) copy-start(f32[256]{0:T(256)} %param.24) | copy-start | bytes 3076
  61.8 13.2 %copy-start.5 = (u32[128]{0:T(128)S(1)}, u32[128]{0:T(128)}, u32[]{:S(2)}) copy-start(u32[128]{0:T(128)} %constant.482) | copy-start | bytes 1540
  61.8 324.0 %all-gather.14.cloned.1.call-start = ((), (), s32[]{:S(2)}) async-start(), calls=%async_computation.2 | async-start | bytes 4325376 | tf_op jit(solution)/shard_map/all_gather | solution.py:97
  220.1 10.3 %collective-permute-start = (f32[256,2]{0,1:T(2,128)S(1)}, f32[256,2]{0,1:T(2,128)S(1)}, u32[]{:S(2)}, u32[]{:S(2)}) collective-permute-start(f32[256,2]{0,1:T(2,128)S(1)} %slice.1874), channel_id=1, source_target_pairs={{0,4},{4,8},{8,12},{1,5},{5,9},{9,13},{2,6},{6,10},{10,14},{3,7},{... | collective-permute-start | bytes 6152 | tf_op jit(solution)/shard_map/ppermute | solution.py:15
  267.0 3.9 collective-permute-start.1
  290.4 5.2 %collective-permute-start.2 = (f32[256,2]{0,1:T(2,128)S(1)}, f32[256,2]{0,1:T(2,128)S(1)}, u32[]{:S(2)}, u32[]{:S(2)}) collective-permute-start(f32[256,2]{0,1:T(2,128)S(1)} %slice.2018), channel_id=1, source_target_pairs={{0,4},{4,8},{8,12},{1,5},{5,9},{9,13},{2,6},{6,10},{10,14},{3,7},{... | collective-permute-start | bytes 6152 | tf_op jit(solution)/shard_map/ppermute | solution.py:15
  315.2 5.2 %collective-permute-start.3 = (f32[256,2]{0,1:T(2,128)S(1)}, f32[256,2]{0,1:T(2,128)S(1)}, u32[]{:S(2)}, u32[]{:S(2)}) collective-permute-start(f32[256,2]{0,1:T(2,128)S(1)} %slice.2064), channel_id=1, source_target_pairs={{0,4},{4,8},{8,12},{1,5},{5,9},{9,13},{2,6},{6,10},{10,14},{3,7},{... | collective-permute-start | bytes 6152 | tf_op jit(solution)/shard_map/ppermute | solution.py:15
  341.0 62.1 %copy-start.1 = (s32[1024]{0:T(1024)S(1)}, s32[1024]{0:T(1024)}, u32[]{:S(2)}) copy-start(s32[1024]{0:T(1024)} %param.20) | copy-start | bytes 12292
Sparse Core Ops, SparseCore 0:
  61.9 84.7 reduce-scatter.1
  341.1 44.6 all-gather.13
where the time goes:
time: 466 us; the launch traced here: 457 us
  blocking collectives  227 us (49%)
  matrix products  92.5 us (20%)
  waiting for transfers between devices  46.8 us (10%)
  local copies, waits for them, and re-layouts  44.1 us (9%)
  between operations  18 us (4%)
  other arithmetic  15.8 us (3%)
  starting transfers between devices  12 us (3%)
    unnamed x1, blocking collectives  128 us
    all_gather x12, blocking collectives, prefix_2(): pieces = jax.tree.map(lambda part: lax.all_gather(part, axis), value)  99.1 us
    all_gather x1, waiting for transfers between devices, shards(): every_trace = lax.all_gather(calcium, ('tile', 'plane'), axis=0, tiled=True)  43 us
    dot_general x16, matrix products, voxel_group(): jnp.einsum('bge,et->bgt', weighted, rows_rounded, preferred_element_type=...  33.2 us
    gather x1, local copies, waits for them, and re-layouts, shards(): gathered = jnp.take(movie, entry_block, axis=0)  24.4 us
    dot_general x1, matrix products, shards(): entry_rows = jnp.dot(member, every_trace, precision=HIGH)  17.3 us
    dot_general x1, matrix products, shards(): partial_energy = jnp.dot(member.T, energy_terms, precision=HIGH)  14.6 us
    dot_general x1, matrix products, shards(): jnp.einsum('ev,evf->ef', footprint, gathered, preferred_element_type=jnp....  14.1 us
  transfers between devices with their start and end apart: 6, of which 4 were waited for; matrix products, arithmetic and copies ran while one was open for 4% of the time, Pallas kernels for 0%

commit v1 on v0

v1 whole, which is shorter than its diff:
```python
import jax
import jax.numpy as jnp
from jax import lax
from jax.experimental import pallas as pl
from jax.experimental.pallas import tpu as pltpu
from jax.sharding import PartitionSpec as P

SWEEPS = 4
CAP = 96
OWN = 256
ENT = 1024
VOX = 128
FR = 128
BLK = 256
MSG = 4 * CAP
ROWS = MSG + 8
SUB = OWN // 4
PIECE = SUB + 8
MESH = pl.DeviceIdType.MESH
F32 = jnp.float32
BF16 = jnp.bfloat16
VMEM = pl.BlockSpec(memory_space=pltpu.VMEM)
SMEM = pl.BlockSpec(memory_space=pltpu.SMEM)
NT = (((1,), (1,)), ((), ()))
TN = (((0,), (0,)), ((), ()))


def iota(shape, axis):
    return lax.broadcasted_iota(jnp.int32, shape, axis)


def split(value):
    high = value.astype(BF16)
    return high, (value - high.astype(F32)).astype(BF16)


def gather_kernel(
    movie_hbm, foot, block_s, block, owner, slot,
    send, pos_out, rank_out, foot_sorted, block_sorted, starts,
    movie, pos_s, sem,
):
    load = pltpu.make_async_copy(movie_hbm, movie, sem.at[0])
    load.start()
    send[...] = jnp.zeros_like(send)
    blk, own, slt = block[...], owner[...], slot[...]
    entry = iota((8, 128), 0) * 128 + iota((8, 128), 1)
    key = (blk * ENT + entry).astype(F32)
    ownf = own.astype(F32)
    key_col, own_col = key.T, ownf.T
    before = iota((128, 128), 0) < iota((128, 128), 1)
    owner_rank, block_rank = [], []
    for row in range(8):
        key_row, own_row = key[row : row + 1, :], ownf[row : row + 1, :]
        count_o = jnp.zeros((128, 128), F32)
        count_k = jnp.zeros((128, 128), F32)
        for col in range(8):
            count_k += jnp.where(key_col[:, col : col + 1] < key_row, 1.0, 0.0)
            if col <= row:
                same = own_col[:, col : col + 1] == own_row
                if col == row:
                    same = same & before
                count_o += jnp.where(same, 1.0, 0.0)
        owner_rank.append(jnp.sum(count_o, axis=0, keepdims=True))
        block_rank.append(jnp.sum(count_k, axis=0, keepdims=True))
    rank = jnp.concatenate(owner_rank, axis=0).astype(jnp.int32)
    order = jnp.concatenate(block_rank, axis=0).astype(jnp.int32)
    core, far, near = (own >> 2) & 1, own >> 3, own & 3
    message = jnp.where(core == 0, far, 4 + near)
    member = jnp.where(core == 0, near, far)
    pos = message * ROWS + member * CAP + rank
    pos_out[...] = pos
    rank_out[...] = order
    to_smem = pltpu.make_async_copy(pos_out, pos_s, sem.at[1])
    to_smem.start()

    foot_values = foot[...].astype(F32)
    sq_high, sq_low = split(foot_values * foot_values)
    ones = jnp.ones((8, 128), BF16)
    energy = lax.dot_general(ones, sq_high, NT, preferred_element_type=F32) + lax.dot_general(
        ones, sq_low, NT, preferred_element_type=F32
    )
    place = member * 128 + rank
    meta = jnp.zeros((24, 512), F32)
    sorted_wide = jnp.zeros((ENT, 256), F32)
    blkf_col = blk.astype(F32).T
    less = jnp.zeros((128, 128), F32)
    lane8 = (iota((128, 128), 1) * 8).astype(F32)
    for row in range(8):
        lanes = slice(row * 128, row * 128 + 128)
        chosen = message[row : row + 1, :] == iota((8, 128), 0)
        en_high, en_low = split(energy[:, lanes])
        slots = (slt[row : row + 1, :] + 1).astype(F32)
        values = jnp.concatenate(
            [
                jnp.where(chosen, slots, 0.0),
                jnp.where(chosen, en_high.astype(F32), 0.0),
                jnp.where(chosen, en_low.astype(F32), 0.0),
            ],
            axis=0,
        ).astype(BF16)
        places = jnp.where(place[row : row + 1, :] == iota((512, 128), 0), 1.0, 0.0).astype(BF16)
        meta += lax.dot_general(values, places, NT, preferred_element_type=F32)
        permute = jnp.where(order[row : row + 1, :] == iota((ENT, 128), 0), 1.0, 0.0).astype(BF16)
        column = blkf_col[:, row : row + 1]
        wide = jnp.concatenate(
            [foot[lanes, :], jnp.broadcast_to(column, (128, 128)).astype(BF16)], axis=1
        )
        sorted_wide += jnp.dot(permute, wide, preferred_element_type=F32)
        less += jnp.where(column < lane8, 1.0, 0.0)
    foot_sorted[...] = sorted_wide[:, :128].astype(BF16)
    block_sorted[...] = sorted_wide[:, 128:]
    starts[...] = jnp.broadcast_to(jnp.sum(less, axis=0, keepdims=True), (8, 128)).astype(jnp.int32)
    for m in range(8):
        for i in range(4):
            lanes = slice(i * 128, i * 128 + 128)
            base = m * ROWS + MSG
            send[base + i : base + i + 1, :] = meta[m : m + 1, lanes]
            send[base + 4 + i : base + 5 + i, :] = (
                meta[8 + m : 9 + m, lanes] + meta[16 + m : 17 + m, lanes]
            )
    to_smem.wait()
    load.wait()
    diagonal = iota((16, 128), 0)

    @pl.loop(0, ENT // 16)
    def _(group):
        first = group * 16
        values = foot[pl.ds(pl.multiple_of(first, 16), 16), :].astype(F32)
        left = jnp.concatenate(
            [jnp.where(diagonal == i, values, 0.0) for i in range(16)], axis=1
        ).astype(BF16)
        right = jnp.concatenate([movie[block_s[first + i]] for i in range(16)], axis=0)
        out = jnp.dot(left, right, preferred_element_type=F32)
        for i in range(16):
            send[pl.ds(pos_s[group // 8, lax.rem(group, 8) * 16 + i], 1), :] = out[i : i + 1, :]


def gather(movie, footprint, entry_block, entry_owner, entry_slot):
    shape = jax.ShapeDtypeStruct
    return pl.pallas_call(
        gather_kernel,
        out_shape=(
            shape((8 * ROWS, FR), F32),
            shape((8, 128), jnp.int32),
            shape((8, 128), jnp.int32),
            shape((ENT, VOX), BF16),
            shape((ENT, 128), F32),
            shape((8, 128), jnp.int32),
        ),
        in_specs=[pl.BlockSpec(memory_space=pl.ANY), VMEM, SMEM, VMEM, VMEM, VMEM],
        out_specs=(VMEM,) * 6,
        scratch_shapes=[
            pltpu.VMEM((BLK, VOX, FR), BF16),
            pltpu.SMEM((8, 128), jnp.int32),
            pltpu.SemaphoreType.DMA((2,)),
        ],
        compiler_params=pltpu.CompilerParams(vmem_limit_bytes=48 << 20),
        name="project",
    )(
        movie, footprint, entry_block, entry_block.reshape(8, 128),
        entry_owner.reshape(8, 128), entry_slot.reshape(8, 128),
    )


def pick(rows, sub):
    chosen = jnp.where(sub // 2 == 0, rows[0:1, :], rows[1:2, :])
    lane = iota((SUB, 128), 1) - lax.rem(sub, 2) * SUB
    return jnp.sum(jnp.where(lane == iota((SUB, 128), 0), chosen, 0.0), axis=1, keepdims=True)


def delayed(parts, steps):
    if steps >= 128:
        hop = steps // 128
        return [None] * hop + parts[: len(parts) - hop]
    lane = iota((SUB, 128), 1)
    rolled = [pltpu.roll(part, steps, 1) for part in parts]
    out = [jnp.where(lane < steps, 0.0, rolled[0])]
    for index in range(1, len(parts)):
        out.append(jnp.where(lane < steps, rolled[index - 1], rolled[index]))
    return out


def first_order(parts, powers):
    for level, power in enumerate(powers):
        moved = delayed(parts, 1 << level)
        parts = [
            part if late is None else part + power * late for part, late in zip(parts, moved)
        ]
    return parts


def sweeps(target, slow, fast):
    lag_one, lag_two = slow + fast, -slow * fast
    slow_powers, fast_powers = [slow], [fast]
    for _ in range(8):
        slow_powers.append(slow_powers[-1] * slow_powers[-1])
        fast_powers.append(fast_powers[-1] * fast_powers[-1])
    slow_share = slow / (slow - fast)
    fast_share = fast / (slow - fast)
    estimate = target
    for sweep in range(SWEEPS):
        one, two = delayed(estimate, 1), delayed(estimate, 2)
        spikes = [
            jnp.maximum(now - lag_one * a - lag_two * b, 0.0)
            for now, a, b in zip(estimate, one, two)
        ]
        slow_part = first_order(spikes, slow_powers)
        fast_part = first_order(spikes, fast_powers)
        calcium = [slow_share * a - fast_share * b for a, b in zip(slow_part, fast_part)]
        if sweep + 1 < SWEEPS:
            estimate = [0.5 * (a + b) for a, b in zip(target, calcium)]
    return calcium


def exchange_kernel(
    send, traces, slow, fast, back, calcium,
    got, hot, part, parts, piece, whole, reply, answer,
    s1, r1, s2, r2, s3, r3, s4, r4, local,
):
    tile, y, z = lax.axis_index("tile"), lax.axis_index("tm"), lax.axis_index("plane")
    x, c = tile // 2, lax.rem(tile, 2)
    d = 1 - c
    p = x * d + z * c
    q = z * d + x * c

    def turn(value, by):
        return lax.rem(value + by, 4)

    def mine(pos, core):
        return (d * (2 * pos + core) + c * (2 * x + core), y, d * z + c * pos)

    def other(pos):
        return (c * 2 * pos + d * (2 * x + 1), y, c * z + d * pos)

    def column(pos, frame):
        return (d * 2 * x + c * (2 * pos + 1), frame, d * pos + c * z)

    far = [(dq, dy) for dq in range(4) for dy in range(4) if (dq, dy) != (0, 0)]
    far = sorted(far, key=lambda pair: -(min(pair[0], 4 - pair[0]) + min(pair[1], 4 - pair[1])))
    reach = (2, 1, 3)

    barrier = pltpu.get_barrier_semaphore()
    met = [mine(turn(p, by), c) for by in reach]
    met += [mine(turn(p, by), d) for by in (2, 1, 3, 0)]
    met += [other(turn(q, by)) for by in reach]
    met += [column(turn(q, dq), turn(y, dy)) for dq, dy in far]
    for device in met:
        pl.semaphore_signal(barrier, inc=1, device_id=device, device_id_type=MESH)
    for source in range(8):
        got[source, ROWS:, :] = jnp.zeros((24, FR), F32)
    part[...] = jnp.zeros_like(part)
    for sub in range(4):
        part[q, sub, :SUB, :] = traces[sub * SUB : (sub + 1) * SUB, :]
    pl.semaphore_wait(barrier, len(met))

    def remote(source, target, sends, arrives, device):
        return pltpu.make_async_remote_copy(
            src_ref=source, dst_ref=target, send_sem=sends, recv_sem=arrives,
            device_id=device, device_id_type=MESH,
        )

    def message(index):
        return send.at[pl.ds(pl.multiple_of(index * ROWS, 8), ROWS), :]

    def landing(index):
        return got.at[index, pl.ds(0, ROWS), :]

    started = []
    own = pltpu.make_async_copy(message(c * 4 + p), landing(p * 2 + c), local.at[0])
    own.start()
    for by in reach:
        index = c * 4 + turn(p, by)
        started.append(
            remote(message(index), landing(p * 2 + c), s1.at[index], r1.at[p * 2 + c], mine(turn(p, by), c))
        )
        started[-1].start()
        index = d * 4 + turn(q, by)
        started.append(
            remote(message(index), landing(q * 2 + c), s1.at[index], r1.at[q * 2 + c], other(turn(q, by)))
        )
        started[-1].start()
    index = d * 4 + q
    started.append(remote(message(index), landing(q * 2 + c), s1.at[index], r1.at[q * 2 + c], other(q)))
    started[-1].start()

    slots_iota = (iota((OWN, 128), 0) + 1).astype(F32)
    weight = [jnp.zeros((OWN, 128), F32) for _ in range(4)]
    own.wait()
    sources = [(0, 0), (0, 1), (1, 0), (1, 1), (3, 0), (3, 1), (2, 0), (2, 1)]
    for by, flip in sources:
        source = turn(p, by) * 2 + (d if flip else c)
        if (by, flip) != (0, 0):
            remote(
                message(0), landing(source), s1.at[0], r1.at[source], mine(turn(p, by), c)
            ).wait_recv()
        for i in range(4):
            slots = got[source, MSG + i : MSG + i + 1, :]
            energies = got[source, MSG + 4 + i : MSG + 5 + i, :]
            match = slots_iota == slots
            chosen = jnp.where(match, 1.0, 0.0).astype(BF16)
            hot[source, i] = chosen
            weight[i] = weight[i] + jnp.where(match, energies, 0.0)
            high, low = split(got[source, i * CAP : i * CAP + 128, :])
            total = jnp.dot(
                jnp.concatenate([chosen, chosen], axis=1),
                jnp.concatenate([high, low], axis=0),
                preferred_element_type=F32,
            )
            for sub in range(4):
                part[i, sub, :SUB, :] += total[sub * SUB : (sub + 1) * SUB, :]
    ones = jnp.ones((8, 128), BF16)
    top = iota((8, 128), 0) == 0
    for i in range(4):
        high, low = split(weight[i])
        energy = lax.dot_general(ones, high, NT, preferred_element_type=F32) + lax.dot_general(
            ones, low, NT, preferred_element_type=F32
        )
        tile_rows = jnp.where(top, energy[:, :128], energy[:, 128:])
        for sub in range(4):
            part[i, sub, SUB:, :] = tile_rows

    for dq, dy in far:
        tq, ty = turn(q, dq), turn(y, dy)
        started.append(
            remote(part.at[tq, ty], parts.at[q, y], s2.at[tq * 4 + ty], r2.at[q * 4 + y], column(tq, ty))
        )
        started[-1].start()
    own = pltpu.make_async_copy(part.at[q, y], parts.at[q, y], local.at[1])
    own.start()
    own.wait()
    for dq, dy in far:
        fq, fy = turn(q, dq), turn(y, dy)
        remote(part.at[0, 0], parts.at[fq, fy], s2.at[0], r2.at[fq * 4 + fy], column(fq, fy)).wait_recv()
    energy = parts[0, 0, SUB : SUB + 2, :]
    for other_q in range(1, 4):
        energy = energy + parts[other_q, 0, SUB : SUB + 2, :]
    scale = pick(energy, y) + 1.0
    target = []
    for frame in range(4):
        total = parts[0, frame, :SUB, :]
        for other_q in range(1, 4):
            total = total + parts[other_q, frame, :SUB, :]
        target.append(total / scale)
    traced = sweeps(target, pick(slow[...], y), pick(fast[...], y))
    for frame in range(4):
        piece[frame] = traced[frame]

    for dq, dy in far:
        tq, ty = turn(q, dq), turn(y, dy)
        started.append(
            remote(piece.at[ty], whole.at[q, y], s3.at[tq * 4 + ty], r3.at[q * 4 + y], column(tq, ty))
        )
        started[-1].start()
    own = pltpu.make_async_copy(piece.at[y], whole.at[q, y], local.at[2])
    own.start()
    own.wait()
    for dq, dy in far:
        fq, fy = turn(q, dq), turn(y, dy)
        remote(piece.at[0], whole.at[fq, fy], s3.at[0], r3.at[fq * 4 + fy], column(fq, fy)).wait_recv()
    for sub in range(4):
        calcium[sub * SUB : (sub + 1) * SUB, :] = whole[q, sub]
    rows = [whole[i].reshape(OWN, FR).astype(BF16) for i in range(4)]

    for by, flip in sources[::-1]:
        core = d if flip else c
        source = turn(p, by) * 2 + core
        for i in range(4):
            got_rows = lax.dot_general(hot[source, i], rows[i], TN, preferred_element_type=F32)
            reply[source, i * CAP : (i + 1) * CAP, :] = got_rows[:CAP, :]
        if (by, flip) == (0, 0):
            own = pltpu.make_async_copy(reply.at[source], answer.at[c * 4 + p], local.at[3])
            own.start()
        else:
            started.append(
                remote(
                    reply.at[source], answer.at[c * 4 + p], s4.at[source], r4.at[c * 4 + p],
                    mine(turn(p, by), core),
                )
            )
            started[-1].start()
    own.wait()
    back[pl.ds(pl.multiple_of((c * 4 + p) * ROWS, 8), MSG), :] = answer[c * 4 + p]
    for by in (0, 1, 3, 2):
        for core, pos in ((d, turn(q, by)), (c, turn(p, by))):
            if by == 0 and core is c:
                continue
            index = core * 4 + pos
            remote(reply.at[0], answer.at[index], s4.at[0], r4.at[index], other(q)).wait_recv()
            back[pl.ds(pl.multiple_of(index * ROWS, 8), MSG), :] = answer[index]
    for copy in started:
        copy.wait_send()


def exchange(send, traces, slow_root, fast_root):
    dma = pltpu.SemaphoreType.DMA
    return pl.pallas_call(
        exchange_kernel,
        out_shape=(
            jax.ShapeDtypeStruct((8 * ROWS, FR), F32),
            jax.ShapeDtypeStruct((OWN, FR), F32),
        ),
        in_specs=[VMEM] * 4,
        out_specs=(VMEM, VMEM),
        scratch_shapes=[
            pltpu.VMEM((8, MSG + 32, FR), F32),
            pltpu.VMEM((8, 4, OWN, 128), BF16),
            pltpu.VMEM((4, 4, PIECE, FR), F32),
            pltpu.VMEM((4, 4, PIECE, FR), F32),
            pltpu.VMEM((4, SUB, FR), F32),
            pltpu.VMEM((4, 4, SUB, FR), F32),
            pltpu.VMEM((8, MSG, FR), F32),
            pltpu.VMEM((8, MSG, FR), F32),
            dma((8,)), dma((8,)), dma((16,)), dma((16,)),
            dma((16,)), dma((16,)), dma((8,)), dma((8,)), dma((4,)),
        ],
        compiler_params=pltpu.CompilerParams(
            collective_id=1, has_side_effects=True, vmem_limit_bytes=48 << 20
        ),
        name="exchange",
    )(send, traces, slow_root.reshape(2, 128), fast_root.reshape(2, 128))


def rebuild_kernel(pos, order, starts, back, foot, block, calcium, out, calcium_out, rows, total):
    step = pl.program_id(0)

    @pl.when(step == 0)
    def _():
        calcium_out[...] = calcium[...]

        @pl.loop(0, ENT // 16)
        def _(group):
            line, lane = group // 8, lax.rem(group, 8) * 16
            for i in range(16):
                rows[pl.ds(order[line, lane + i], 1), :] = back[pl.ds(pos[line, lane + i], 1), :]

    begin, end = starts[0, step], starts[0, step + 1]
    first = jnp.minimum(begin // 128, ENT // 128 - 1)
    last = jnp.maximum(first, (end - 1) // 128)

    def product(window):
        span = pl.ds(pl.multiple_of(window * 128, 128), 128)
        values, which = rows[span, :], block[span, :]
        masked = jnp.concatenate(
            [
                jnp.where(which == (step * 8 + n).astype(F32), values, 0.0).astype(BF16)
                for n in range(8)
            ],
            axis=1,
        )
        return lax.dot_general(foot[span, :], masked, TN, preferred_element_type=F32)

    def store(result):
        for n in range(8):
            out[n] = result[:, n * 128 : (n + 1) * 128].astype(BF16)

    @pl.when(first == last)
    def _():
        store(product(first))

    @pl.when(first != last)
    def _():
        total[...] = product(first)

        @pl.loop(first + 1, last + 1)
        def _(window):
            total[...] += product(window)

        store(total[...])


def rebuild(pos, order, starts, back, foot, block, calcium):
    grid = BLK // 8
    whole = lambda shape: pl.BlockSpec(shape, lambda i: (0, 0))
    return pl.pallas_call(
        rebuild_kernel,
        grid=(grid,),
        out_shape=(
            jax.ShapeDtypeStruct((BLK, VOX, FR), BF16),
            jax.ShapeDtypeStruct((OWN, FR), F32),
        ),
        in_specs=[SMEM, SMEM, SMEM, whole((8 * ROWS, FR)), whole((ENT, VOX)), whole((ENT, 128)), whole((OWN, FR))],
        out_specs=(pl.BlockSpec((8, VOX, FR), lambda i: (i, 0, 0)), whole((OWN, FR))),
        scratch_shapes=[pltpu.VMEM((ENT, FR), F32), pltpu.VMEM((VOX, 8 * FR), F32)],
        compiler_params=pltpu.CompilerParams(vmem_limit_bytes=32 << 20),
        name="rebuild",
    )(pos, order, starts, back, foot, block, calcium)


def shards(movie, footprint, entry_block, entry_owner, entry_slot, traces, slow_root, fast_root):
    send, pos, order, foot, block, starts = gather(
        movie, footprint, entry_block, entry_owner, entry_slot
    )
    back, calcium = exchange(send, traces, slow_root, fast_root)
    return rebuild(pos, order, starts, back, foot, block, calcium)


def solution(mesh):
    owners = ("tile", "plane")
    placed = (
        P(owners, None, "tm"),
        P(owners, None),
        P(owners),
        P(owners, None),
        P(owners),
        P(owners, "tm"),
        P(owners),
        P(owners),
    )
    return jax.shard_map(
        shards,
        mesh=mesh,
        in_specs=placed,
        out_specs=(P(owners, None, "tm"), P(owners, "tm")),
        check_vma=False,
    )
```

time: 466 us -> 93.8 us (0.20); the launches traced: 457 us -> 93.5 us
  blocking collectives: 227 us -> 0 us
  matrix products: 92.5 us -> 0 us
  Pallas kernels: 0 us -> 89.8 us
  waiting for transfers between devices: 46.8 us -> 0 us
  local copies, waits for them, and re-layouts: 44.1 us -> 3.03 us
  between operations: 18 us -> 0.7 us
  other arithmetic: 15.8 us -> 0 us
  starting transfers between devices: 12 us -> 0 us
    unnamed x1 -> x0, blocking collectives: 128 us -> none
    all_gather x12 -> x0, blocking collectives: 99.1 us -> none  [prefix_2(): pieces = jax.tree.map(lambda part: lax.all_gather(part, axis), value)]
    dot_general x20 -> x0, matrix products: 92.5 us -> none  [the longest x16 33.2 us: voxel_group(): jnp.einsum('bge,et->bgt', weighted, rows_rounded, preferred_element_type=...]
    pallas_call x0 -> x3, Pallas kernels: none -> 89.8 us  [the longest x1 51 us: exchange(): pl.pallas_call(exchange_kernel, out_shape=(jax.ShapeDtypeStruct((8 * ROWS...]
    all_gather x1 -> x0, waiting for transfers between devices: 43 us -> none  [shards(): every_trace = lax.all_gather(calcium, ('tile', 'plane'), axis=0, tiled=True)]
    gather x1 -> x0, local copies, waits for them, and re-layouts: 24.4 us -> none  [shards(): gathered = jnp.take(movie, entry_block, axis=0)]
    convert_element_type x1 -> x0, local copies, waits for them, and re-layouts: 12.2 us -> none  [shards(): return (rebuilt.astype(jnp.bfloat16), calcium)]
    ppermute x4 -> x0, starting transfers between devices: 11.9 us -> none  [shifted(): lax.ppermute(value, axis, [(source, source + steps) for source in range(l...]
  transfers between devices with their start and end apart: 6 -> 0, of which waited for: 4 -> 0; matrix products, arithmetic and copies ran while one was open for 4% -> 0% of each run, Pallas kernels for 0% -> 0%
where the time goes in v1:
time: 93.8 us; the launch traced here: 93.5 us
  Pallas kernels  89.8 us (96%)
  local copies, waits for them, and re-layouts  3.03 us (3%)
    pallas_call x1, Pallas kernels, exchange(): pl.pallas_call(exchange_kernel, out_shape=(jax.ShapeDtypeStruct((8 * ROWS...  51 us
    pallas_call x1, Pallas kernels, rebuild(): pl.pallas_call(rebuild_kernel, grid=(grid,), out_shape=(jax.ShapeDtypeStr...  22.1 us
    pallas_call x1, Pallas kernels, gather(): pl.pallas_call(gather_kernel, out_shape=(shape((8 * ROWS, FR), F32), shap...  16.7 us
    unnamed x14, local copies, waits for them, and re-layouts  3.03 us

profile of v1, /device:TPU:0, one launch (start us, length us, event | category | flops | bytes accessed | tf_op | source)
XLA Modules:
  0.0 93.5 jit_solution(14648907954166450703)
XLA Ops:
  0.6 0.0 copy-start.6
  0.6 0.0 copy-start.5
  0.7 0.0 copy-start
  0.7 1.0 %copy-done = bf16[1024,128]{1,0:T(8,128)(2,1)S(1)} copy-done((bf16[1024,128]{1,0:T(8,128)(2,1)S(1)}, bf16[1024,128]{1,0:T(8,128)(2,1)}, u32[]{:S(2)}) %copy-start) | copy-done | bytes 262168
  1.6 0.0 copy-start.2
  1.6 0.7 copy-done.2
  2.3 0.0 copy-start.3
  2.3 0.7 copy-done.3
  3.0 0.0 copy-start.4
  3.0 0.7 copy-done.4
  3.7 0.0 copy-start.1
  3.7 16.7 %project.1 = (f32[3136,128]{1,0:T(8,128)S(1)}, s32[8,128]{1,0:T(8,128)S(1)}, s32[8,128]{1,0:T(8,128)S(1)}, bf16[1024,128]{1,0:T(8,128)(2,1)S(1)}, f32[1024,128]{1,0:T(8,128)S(1)}, /*index=5*/s32[8,128]{1,0:T(8,128)S(1)}) custom-call(bf16[256,128,128]{2,1,0:T(8,128)(2,1)} %movie_hbm.1, bf16[1024,128]{1,0:T(8,128)(2,1)S(1)} %copy-done, s32[1024]{0:T(1024)S(1)} %copy-done.2, ...), custom_call_target="tpu_custom_call" | custom-call | tf_op jit(solution)/shard_map/project/pallas_call | solution.py:140
  20.4 0.0 copy-done.6
  20.4 0.0 copy-done.5
  20.5 0.0 copy-done.1
  20.5 51.0 %exchange.1 = (f32[3136,128]{1,0:T(8,128)S(1)}, f32[256,128]{1,0:T(8,128)S(1)}) custom-call(f32[3136,128]{1,0:T(8,128)S(1)} %get-tuple-element.13.send, f32[256,128]{1,0:T(8,128)S(1)} %copy-done.1, f32[2,128]{1,0:T(2,128)S(1)} %bitcast.8, f32[2,128]{1,0:T(2,128)S(1)} %bitcast.9), custom_call_target="tpu_custom_call" | custom-call | tf_op jit(solution)/shard_map/exchange/pallas_call | solution.py:396
  71.4 22.1 %rebuild.1 = (bf16[256,128,128]{2,1,0:T(8,128)(2,1)}, f32[256,128]{1,0:T(8,128)}) custom-call(s32[8,128]{1,0:T(8,128)S(1)} %get-tuple-element.10.pos, s32[8,128]{1,0:T(8,128)S(1)} %get-tuple-element.11.order, s32[8,128]{1,0:T(8,128)S(1)} %get-tuple-element.12.starts, f32[3136,128]{1,0:T(8,128)S(1)} %get-tuple-element.14.back, ...), custom_call_target="tpu_custom_call" | custom-call | tf_op jit(solution)/shard_map/rebuild/pallas_call | solution.py:474
Async XLA Ops:
  0.6 19.8 %copy-start.6 = (f32[256]{0:T(256)S(1)}, f32[256]{0:T(256)}, u32[]{:S(2)}) copy-start(f32[256]{0:T(256)} %param.15) | copy-start | bytes 3076
  0.6 19.8 %copy-start.5 = (f32[256]{0:T(256)S(1)}, f32[256]{0:T(256)}, u32[]{:S(2)}) copy-start(f32[256]{0:T(256)} %param.14) | copy-start | bytes 3076
  0.7 1.0 %copy-start = (bf16[1024,128]{1,0:T(8,128)(2,1)S(1)}, bf16[1024,128]{1,0:T(8,128)(2,1)}, u32[]{:S(2)}) copy-start(bf16[1024,128]{1,0:T(8,128)(2,1)} %foot.1) | copy-start | bytes 786436
  1.6 0.7 copy-start.2
  2.3 0.7 copy-start.3
  3.0 0.7 copy-start.4
  3.7 16.8 %copy-start.1 = (f32[256,128]{1,0:T(8,128)S(1)}, f32[256,128]{1,0:T(8,128)}, u32[]{:S(2)}) copy-start(f32[256,128]{1,0:T(8,128)} %traces.1) | copy-start | bytes 393220

commit v2 on v1

--- a/solution.py
+++ b/solution.py
@@ -16,6 +16,8 @@
 ROWS = MSG + 8
 SUB = OWN // 4
 PIECE = SUB + 8
+WINDOW = 64
+PART = 64
 MESH = pl.DeviceIdType.MESH
 F32 = jnp.float32
 BF16 = jnp.bfloat16
@@ -35,20 +37,40 @@
 
 
 def gather_kernel(
-    movie_hbm, foot, block_s, block, owner, slot,
-    send, pos_out, rank_out, foot_sorted, block_sorted, starts,
-    movie, pos_s, sem,
+    movie_hbm, foot_hbm, block_hbm, owner_hbm, slot_hbm,
+    send, pos_out, rank_out, starts_out, foot_sorted, block_sorted,
+    movie, foot, index, projected, pos_s, rank_s, starts_s, sem, movie_sem,
 ):
-    load = pltpu.make_async_copy(movie_hbm, movie, sem.at[0])
-    load.start()
+    small = [
+        pltpu.make_async_copy(source, target, sem.at[number])
+        for number, (source, target) in enumerate(
+            [(block_hbm, index.at[0]), (owner_hbm, index.at[1]), (slot_hbm, index.at[2]), (foot_hbm, foot)]
+        )
+    ]
+    for copy in small:
+        copy.start()
+
+    def movie_part(number):
+        span = pl.ds(number * PART, PART)
+        return pltpu.make_async_copy(movie_hbm.at[span], movie.at[span], movie_sem.at[number])
+
+    for number in range(BLK // PART):
+        movie_part(number).start()
     send[...] = jnp.zeros_like(send)
-    blk, own, slt = block[...], owner[...], slot[...]
+    projected[...] = jnp.zeros_like(projected)
+    foot_sorted[ENT:, :] = jnp.zeros((WINDOW, VOX), F32)
+    block_sorted[ENT:, :] = jnp.full((WINDOW, 128), -1.0, F32)
+    for copy in small:
+        copy.wait()
+    blk, own, slt = index[0], index[1], index[2]
     entry = iota((8, 128), 0) * 128 + iota((8, 128), 1)
     key = (blk * ENT + entry).astype(F32)
     ownf = own.astype(F32)
-    key_col, own_col = key.T, ownf.T
+    key_col, own_col, blk_col = key.T, ownf.T, blk.astype(F32).T
     before = iota((128, 128), 0) < iota((128, 128), 1)
+    lane8 = (iota((128, 128), 1) * 8).astype(F32)
     owner_rank, block_rank = [], []
+    less = jnp.zeros((128, 128), F32)
     for row in range(8):
         key_row, own_row = key[row : row + 1, :], ownf[row : row + 1, :]
         count_o = jnp.zeros((128, 128), F32)
@@ -62,16 +84,25 @@
                 count_o += jnp.where(same, 1.0, 0.0)
         owner_rank.append(jnp.sum(count_o, axis=0, keepdims=True))
         block_rank.append(jnp.sum(count_k, axis=0, keepdims=True))
+        less += jnp.where(blk_col[:, row : row + 1] < lane8, 1.0, 0.0)
     rank = jnp.concatenate(owner_rank, axis=0).astype(jnp.int32)
     order = jnp.concatenate(block_rank, axis=0).astype(jnp.int32)
     core, far, near = (own >> 2) & 1, own >> 3, own & 3
     message = jnp.where(core == 0, far, 4 + near)
     member = jnp.where(core == 0, near, far)
-    pos = message * ROWS + member * CAP + rank
-    pos_out[...] = pos
+    pos_out[...] = message * ROWS + member * CAP + rank
     rank_out[...] = order
-    to_smem = pltpu.make_async_copy(pos_out, pos_s, sem.at[1])
-    to_smem.start()
+    starts_out[...] = jnp.broadcast_to(jnp.sum(less, axis=0, keepdims=True), (8, 128)).astype(
+        jnp.int32
+    )
+    to_smem = [
+        pltpu.make_async_copy(source, target, sem.at[4 + number])
+        for number, (source, target) in enumerate(
+            [(pos_out, pos_s), (rank_out, rank_s), (starts_out, starts_s)]
+        )
+    ]
+    for copy in to_smem:
+        copy.start()
 
     foot_values = foot[...].astype(F32)
     sq_high, sq_low = split(foot_values * foot_values)
@@ -82,9 +113,6 @@
     place = member * 128 + rank
     meta = jnp.zeros((24, 512), F32)
     sorted_wide = jnp.zeros((ENT, 256), F32)
-    blkf_col = blk.astype(F32).T
-    less = jnp.zeros((128, 128), F32)
-    lane8 = (iota((128, 128), 1) * 8).astype(F32)
     for row in range(8):
         lanes = slice(row * 128, row * 128 + 128)
         chosen = message[row : row + 1, :] == iota((8, 128), 0)
@@ -101,15 +129,16 @@
         places = jnp.where(place[row : row + 1, :] == iota((512, 128), 0), 1.0, 0.0).astype(BF16)
         meta += lax.dot_general(values, places, NT, preferred_element_type=F32)
         permute = jnp.where(order[row : row + 1, :] == iota((ENT, 128), 0), 1.0, 0.0).astype(BF16)
-        column = blkf_col[:, row : row + 1]
         wide = jnp.concatenate(
-            [foot[lanes, :], jnp.broadcast_to(column, (128, 128)).astype(BF16)], axis=1
+            [
+                foot[lanes, :],
+                jnp.broadcast_to(blk_col[:, row : row + 1], (128, 128)).astype(BF16),
+            ],
+            axis=1,
         )
         sorted_wide += jnp.dot(permute, wide, preferred_element_type=F32)
-        less += jnp.where(column < lane8, 1.0, 0.0)
-    foot_sorted[...] = sorted_wide[:, :128].astype(BF16)
-    block_sorted[...] = sorted_wide[:, 128:]
-    starts[...] = jnp.broadcast_to(jnp.sum(less, axis=0, keepdims=True), (8, 128)).astype(jnp.int32)
+    foot_sorted[:ENT, :] = sorted_wide[:, :128]
+    block_sorted[:ENT, :] = sorted_wide[:, 128:]
     for m in range(8):
         for i in range(4):
             lanes = slice(i * 128, i * 128 + 128)
@@ -118,46 +147,92 @@
             send[base + 4 + i : base + 5 + i, :] = (
                 meta[8 + m : 9 + m, lanes] + meta[16 + m : 17 + m, lanes]
             )
-    to_smem.wait()
-    load.wait()
-    diagonal = iota((16, 128), 0)
-
-    @pl.loop(0, ENT // 16)
+    for copy in to_smem:
+        copy.wait()
+
+    def product(chunk, first):
+        span = pl.ds(pl.multiple_of(first, 8), WINDOW)
+        values, which = foot_sorted[span, :], block_sorted[span, :]
+        left = jnp.concatenate(
+            [
+                jnp.where(which == (chunk * 8 + n).astype(F32), values, 0.0).astype(BF16)
+                for n in range(8)
+            ],
+            axis=1,
+        )
+        right = movie[pl.ds(chunk * 8, 8)].reshape(8 * VOX, FR)
+        projected[span, :] += jnp.dot(left, right, preferred_element_type=F32)
+
+    @pl.loop(0, BLK // PART)
     def _(group):
-        first = group * 16
-        values = foot[pl.ds(pl.multiple_of(first, 16), 16), :].astype(F32)
-        left = jnp.concatenate(
-            [jnp.where(diagonal == i, values, 0.0) for i in range(16)], axis=1
-        ).astype(BF16)
-        right = jnp.concatenate([movie[block_s[first + i]] for i in range(16)], axis=0)
-        out = jnp.dot(left, right, preferred_element_type=F32)
-        for i in range(16):
-            send[pl.ds(pos_s[group // 8, lax.rem(group, 8) * 16 + i], 1), :] = out[i : i + 1, :]
+        movie_part(group).wait()
+        windows(starts_s, group, product)
+
+    @pl.loop(0, 8)
+    def _(line):
+        for lane in range(128):
+            send[pl.ds(pos_s[line, lane], 1), :] = projected[pl.ds(rank_s[line, lane], 1), :]
+
+
+def windows(starts, group, product):
+    count = PART // 8
+    fits = None
+    for k in range(count):
+        chunk = group * count + k
+        begin = (starts[0, chunk] // 8) * 8
+        inside = starts[0, chunk + 1] - begin <= WINDOW
+        fits = inside if fits is None else fits & inside
+
+    @pl.when(fits)
+    def _():
+        for k in range(count):
+            chunk = group * count + k
+            product(chunk, (starts[0, chunk] // 8) * 8)
+
+    @pl.when(jnp.logical_not(fits))
+    def _():
+        @pl.loop(0, count)
+        def _(k):
+            chunk = group * count + k
+            begin = (starts[0, chunk] // 8) * 8
+            number = jnp.maximum(1, (starts[0, chunk + 1] - begin + WINDOW - 1) // WINDOW)
+
+            @pl.loop(0, number)
+            def _(step):
+                product(chunk, begin + step * WINDOW)
 
 
 def gather(movie, footprint, entry_block, entry_owner, entry_slot):
     shape = jax.ShapeDtypeStruct
+    any_place = pl.BlockSpec(memory_space=pl.ANY)
+    index = shape((8, 128), jnp.int32)
     return pl.pallas_call(
         gather_kernel,
         out_shape=(
             shape((8 * ROWS, FR), F32),
-            shape((8, 128), jnp.int32),
-            shape((8, 128), jnp.int32),
-            shape((ENT, VOX), BF16),
-            shape((ENT, 128), F32),
-            shape((8, 128), jnp.int32),
+            index,
+            index,
+            index,
+            shape((ENT + WINDOW, VOX), F32),
+            shape((ENT + WINDOW, 128), F32),
         ),
-        in_specs=[pl.BlockSpec(memory_space=pl.ANY), VMEM, SMEM, VMEM, VMEM, VMEM],
+        in_specs=[any_place] * 5,
         out_specs=(VMEM,) * 6,
         scratch_shapes=[
             pltpu.VMEM((BLK, VOX, FR), BF16),
+            pltpu.VMEM((ENT, VOX), BF16),
+            pltpu.VMEM((3, 8, 128), jnp.int32),
+            pltpu.VMEM((ENT + WINDOW, FR), F32),
             pltpu.SMEM((8, 128), jnp.int32),
-            pltpu.SemaphoreType.DMA((2,)),
+            pltpu.SMEM((8, 128), jnp.int32),
+            pltpu.SMEM((8, 128), jnp.int32),
+            pltpu.SemaphoreType.DMA((7,)),
+            pltpu.SemaphoreType.DMA((BLK // PART,)),
         ],
-        compiler_params=pltpu.CompilerParams(vmem_limit_bytes=48 << 20),
+        compiler_params=pltpu.CompilerParams(vmem_limit_bytes=56 << 20),
         name="project",
     )(
-        movie, footprint, entry_block, entry_block.reshape(8, 128),
+        movie, footprint, entry_block.reshape(8, 128),
         entry_owner.reshape(8, 128), entry_slot.reshape(8, 128),
     )
 
@@ -420,74 +495,98 @@
     )(send, traces, slow_root.reshape(2, 128), fast_root.reshape(2, 128))
 
 
-def rebuild_kernel(pos, order, starts, back, foot, block, calcium, out, calcium_out, rows, total):
-    step = pl.program_id(0)
-
-    @pl.when(step == 0)
-    def _():
-        calcium_out[...] = calcium[...]
-
-        @pl.loop(0, ENT // 16)
-        def _(group):
-            line, lane = group // 8, lax.rem(group, 8) * 16
-            for i in range(16):
-                rows[pl.ds(order[line, lane + i], 1), :] = back[pl.ds(pos[line, lane + i], 1), :]
-
-    begin, end = starts[0, step], starts[0, step + 1]
-    first = jnp.minimum(begin // 128, ENT // 128 - 1)
-    last = jnp.maximum(first, (end - 1) // 128)
-
-    def product(window):
-        span = pl.ds(pl.multiple_of(window * 128, 128), 128)
+def rebuild_kernel(
+    pos, order, starts, back, foot, block, calcium, out_hbm, calcium_out, rows, out, total, sem
+):
+    calcium_out[...] = calcium[...]
+    rows[ENT:, :] = jnp.zeros((WINDOW, FR), F32)
+
+    @pl.loop(0, 8)
+    def _(line):
+        for lane in range(128):
+            rows[pl.ds(order[line, lane], 1), :] = back[pl.ds(pos[line, lane], 1), :]
+
+    def product(chunk, first):
+        span = pl.ds(pl.multiple_of(first, 8), WINDOW)
         values, which = rows[span, :], block[span, :]
         masked = jnp.concatenate(
             [
-                jnp.where(which == (step * 8 + n).astype(F32), values, 0.0).astype(BF16)
+                jnp.where(which == (chunk * 8 + n).astype(F32), values, 0.0).astype(BF16)
                 for n in range(8)
             ],
             axis=1,
         )
-        return lax.dot_general(foot[span, :], masked, TN, preferred_element_type=F32)
-
-    def store(result):
+        left = foot[span, :].astype(BF16)
+        return lax.dot_general(left, masked, TN, preferred_element_type=F32)
+
+    def out_part(number):
+        span = pl.ds(number * PART, PART)
+        return pltpu.make_async_copy(out.at[span], out_hbm.at[span], sem.at[number])
+
+    def store(chunk, result):
         for n in range(8):
-            out[n] = result[:, n * 128 : (n + 1) * 128].astype(BF16)
-
-    @pl.when(first == last)
-    def _():
-        store(product(first))
-
-    @pl.when(first != last)
-    def _():
-        total[...] = product(first)
-
-        @pl.loop(first + 1, last + 1)
-        def _(window):
-            total[...] += product(window)
-
-        store(total[...])
+            out[chunk * 8 + n] = result[:, n * FR : (n + 1) * FR].astype(BF16)
+
+    count = PART // 8
+
+    @pl.loop(0, BLK // PART)
+    def _(group):
+        fits = None
+        for k in range(count):
+            chunk = group * count + k
+            inside = starts[0, chunk + 1] - (starts[0, chunk] // 8) * 8 <= WINDOW
+            fits = inside if fits is None else fits & inside
+
+        @pl.when(fits)
+        def _():
+            for k in range(count):
+                chunk = group * count + k
+                store(chunk, product(chunk, (starts[0, chunk] // 8) * 8))
+
+        @pl.when(jnp.logical_not(fits))
+        def _():
+            @pl.loop(0, count)
+            def _(k):
+                chunk = group * count + k
+                begin = (starts[0, chunk] // 8) * 8
+                number = jnp.maximum(1, (starts[0, chunk + 1] - begin + WINDOW - 1) // WINDOW)
+                total[...] = product(chunk, begin)
+
+                @pl.loop(1, number)
+                def _(step):
+                    total[...] += product(chunk, begin + step * WINDOW)
+
+                store(chunk, total[...])
+
+        out_part(group).start()
+
+    @pl.loop(0, BLK // PART)
+    def _(group):
+        out_part(group).wait()
 
 
 def rebuild(pos, order, starts, back, foot, block, calcium):
-    grid = BLK // 8
-    whole = lambda shape: pl.BlockSpec(shape, lambda i: (0, 0))
     return pl.pallas_call(
         rebuild_kernel,
-        grid=(grid,),
         out_shape=(
             jax.ShapeDtypeStruct((BLK, VOX, FR), BF16),
             jax.ShapeDtypeStruct((OWN, FR), F32),
         ),
-        in_specs=[SMEM, SMEM, SMEM, whole((8 * ROWS, FR)), whole((ENT, VOX)), whole((ENT, 128)), whole((OWN, FR))],
-        out_specs=(pl.BlockSpec((8, VOX, FR), lambda i: (i, 0, 0)), whole((OWN, FR))),
-        scratch_shapes=[pltpu.VMEM((ENT, FR), F32), pltpu.VMEM((VOX, 8 * FR), F32)],
-        compiler_params=pltpu.CompilerParams(vmem_limit_bytes=32 << 20),
+        in_specs=[SMEM] * 3 + [VMEM] * 4,
+        out_specs=(pl.BlockSpec(memory_space=pl.ANY), VMEM),
+        scratch_shapes=[
+            pltpu.VMEM((ENT + WINDOW, FR), F32),
+            pltpu.VMEM((BLK, VOX, FR), BF16),
+            pltpu.VMEM((VOX, 8 * FR), F32),
+            pltpu.SemaphoreType.DMA((BLK // PART,)),
+        ],
+        compiler_params=pltpu.CompilerParams(vmem_limit_bytes=48 << 20),
         name="rebuild",
     )(pos, order, starts, back, foot, block, calcium)
 
 
 def shards(movie, footprint, entry_block, entry_owner, entry_slot, traces, slow_root, fast_root):
-    send, pos, order, foot, block, starts = gather(
+    send, pos, order, starts, foot, block = gather(
         movie, footprint, entry_block, entry_owner, entry_slot
     )
     back, calcium = exchange(send, traces, slow_root, fast_root)

time: 93.8 us -> 75.2 us (0.80)
  Pallas kernels: 89.8 us -> 68.6 us
  local copies, waits for them, and re-layouts: 3.03 us -> 5.57 us
    pallas_call x2, Pallas kernels: 38.9 us -> 17.9 us  [the longest x1 10.5 us: gather(): pl.pallas_call(gather_kernel, out_shape=(shape((8 * ROWS, FR), F32), inde...]
    unnamed x14 -> x18, local copies, waits for them, and re-layouts: 3.03 us -> 5.57 us
where the time goes in v2:
time: 75.2 us; the launch traced here: 74.9 us
  Pallas kernels  68.6 us (91%)
  local copies, waits for them, and re-layouts  5.57 us (7%)
    pallas_call x1, Pallas kernels, exchange(): pl.pallas_call(exchange_kernel, out_shape=(jax.ShapeDtypeStruct((8 * ROWS...  50.8 us
    pallas_call x1, Pallas kernels, gather(): pl.pallas_call(gather_kernel, out_shape=(shape((8 * ROWS, FR), F32), inde...  10.5 us
    pallas_call x1, Pallas kernels, rebuild(): pl.pallas_call(rebuild_kernel, out_shape=(jax.ShapeDtypeStruct((BLK, VOX,...  7.32 us
    unnamed x18, local copies, waits for them, and re-layouts  5.57 us

profile of v2, /device:TPU:0, one launch (start us, length us, event | category | flops | bytes accessed | tf_op | source)
XLA Modules:
  0.0 74.9 jit_solution(16495357355106609441)
XLA Ops:
  0.6 0.0 copy-start.8
  0.6 0.0 copy-start.7
  0.7 0.0 copy-start.3
  0.7 10.5 %project.1 = (f32[3136,128]{1,0:T(8,128)}, s32[8,128]{1,0:T(8,128)}, s32[8,128]{1,0:T(8,128)}, s32[8,128]{1,0:T(8,128)}, f32[1088,128]{1,0:T(8,128)}, /*index=5*/f32[1088,128]{1,0:T(8,128)}) custom-call(bf16[256,128,128]{2,1,0:T(8,128)(2,1)} %movie_hbm.1, bf16[1024,128]{1,0:T(8,128)(2,1)} %foot_hbm.1, s32[8,128]{1,0:T(8,128)} %bitcast.7, s32[8,128]{1,0:T(8,128)} %bitcast.8, ...), custom_call_target="tpu_custom_call" | custom-call | tf_op jit(solution)/shard_map/project/pallas_call | solution.py:209
  11.2 0.0 copy-done.8
  11.2 0.0 copy-done.7
  11.2 0.0 copy-done.3
  11.2 0.0 copy-start
  11.3 1.4 %copy-done = f32[3136,128]{1,0:T(8,128)S(1)} copy-done((f32[3136,128]{1,0:T(8,128)S(1)}, f32[3136,128]{1,0:T(8,128)}, u32[]{:S(2)}) %copy-start) | copy-done | bytes 1605656
  12.7 50.8 %exchange.1 = (f32[3136,128]{1,0:T(8,128)S(1)}, f32[256,128]{1,0:T(8,128)S(1)}) custom-call(f32[3136,128]{1,0:T(8,128)S(1)} %copy-done, f32[256,128]{1,0:T(8,128)S(1)} %copy-done.3, f32[2,128]{1,0:T(2,128)S(1)} %bitcast.5, f32[2,128]{1,0:T(2,128)S(1)} %bitcast.6), custom_call_target="tpu_custom_call" | custom-call | tf_op jit(solution)/shard_map/exchange/pallas_call | solution.py:471
  63.4 0.0 copy-start.1
  63.4 1.0 %copy-done.1 = f32[1088,128]{1,0:T(8,128)S(1)} copy-done((f32[1088,128]{1,0:T(8,128)S(1)}, f32[1088,128]{1,0:T(8,128)}, u32[]{:S(2)}) %copy-start.1) | copy-done | bytes 557080
  64.5 0.0 copy-start.2
  64.5 1.1 %copy-done.2 = f32[1088,128]{1,0:T(8,128)S(1)} copy-done((f32[1088,128]{1,0:T(8,128)S(1)}, f32[1088,128]{1,0:T(8,128)}, u32[]{:S(2)}) %copy-start.2) | copy-done | bytes 557080
  65.5 0.0 copy-start.4
  65.5 0.7 copy-done.4
  66.2 0.0 copy-start.5
  66.2 0.7 copy-done.5
  66.9 0.0 copy-start.6
  66.9 0.7 copy-done.6
  67.6 7.3 %rebuild.1 = (bf16[256,128,128]{2,1,0:T(8,128)(2,1)}, f32[256,128]{1,0:T(8,128)}) custom-call(s32[8,128]{1,0:T(8,128)S(1)} %copy-done.4, s32[8,128]{1,0:T(8,128)S(1)} %copy-done.5, s32[8,128]{1,0:T(8,128)S(1)} %copy-done.6, f32[3136,128]{1,0:T(8,128)S(1)} %get-tuple-element.14.back, f32[1088,128]{1,0:T(8,128)S(1)} %copy-done.1, f32[1088,128]{1,0:T(8,128)S(1)} %copy-done.2, ...), custom_call_target="tpu_custom_call" | custom-call | tf_op jit(solution)/shard_map/rebuild/pallas_call | solution.py:569
Async XLA Ops:
  0.6 10.6 %copy-start.8 = (f32[256]{0:T(256)S(1)}, f32[256]{0:T(256)}, u32[]{:S(2)}) copy-start(f32[256]{0:T(256)} %param.15) | copy-start | bytes 3076
  0.6 10.6 %copy-start.7 = (f32[256]{0:T(256)S(1)}, f32[256]{0:T(256)}, u32[]{:S(2)}) copy-start(f32[256]{0:T(256)} %param.14) | copy-start | bytes 3076
  0.7 10.6 %copy-start.3 = (f32[256,128]{1,0:T(8,128)S(1)}, f32[256,128]{1,0:T(8,128)}, u32[]{:S(2)}) copy-start(f32[256,128]{1,0:T(8,128)} %traces.1) | copy-start | bytes 393220
  11.2 1.4 %copy-start = (f32[3136,128]{1,0:T(8,128)S(1)}, f32[3136,128]{1,0:T(8,128)}, u32[]{:S(2)}) copy-start(f32[3136,128]{1,0:T(8,128)} %get-tuple-element.13.send) | copy-start | bytes 4816900
  63.4 1.1 %copy-start.1 = (f32[1088,128]{1,0:T(8,128)S(1)}, f32[1088,128]{1,0:T(8,128)}, u32[]{:S(2)}) copy-start(f32[1088,128]{1,0:T(8,128)} %get-tuple-element.15.foot) | copy-start | bytes 1671172
  64.5 1.1 %copy-start.2 = (f32[1088,128]{1,0:T(8,128)S(1)}, f32[1088,128]{1,0:T(8,128)}, u32[]{:S(2)}) copy-start(f32[1088,128]{1,0:T(8,128)} %get-tuple-element.16.block) | copy-start | bytes 1671172
  65.5 0.7 copy-start.4
  66.2 0.7 copy-start.5
  66.9 0.7 copy-start.6

commit v3 on v2

v3 whole, which is shorter than its diff:
```python
import jax
import jax.numpy as jnp
from jax import lax
from jax.experimental import pallas as pl
from jax.experimental.pallas import tpu as pltpu
from jax.sharding import PartitionSpec as P

SWEEPS = 4
TURNS = (2, 1, 3, 0)
CAP = 96
OWN = 256
ENT = 1024
VOX = 128
FR = 128
BLK = 256
MSG = 4 * CAP
ROWS = MSG + 8
SUB = OWN // 4
PIECE = SUB + 8
WINDOW = 64
PART = 64
MESH = pl.DeviceIdType.MESH
F32 = jnp.float32
BF16 = jnp.bfloat16
VMEM = pl.BlockSpec(memory_space=pltpu.VMEM)
NT = (((1,), (1,)), ((), ()))
TN = (((0,), (0,)), ((), ()))


def iota(shape, axis):
    return lax.broadcasted_iota(jnp.int32, shape, axis)


def split(value):
    high = value.astype(BF16)
    return high, (value - high.astype(F32)).astype(BF16)


def gather_kernel(
    movie_hbm, foot_hbm, block_hbm, owner_hbm, slot_hbm,
    send, numbers, foot_sorted, block_sorted,
    movie, foot, index, projected, numbers_s, sem, movie_sem,
):
    small = [
        pltpu.make_async_copy(source, target, sem.at[number])
        for number, (source, target) in enumerate(
            [(block_hbm, index.at[0]), (owner_hbm, index.at[1]), (slot_hbm, index.at[2]), (foot_hbm, foot)]
        )
    ]
    for copy in small:
        copy.start()

    def movie_part(number):
        span = pl.ds(number * PART, PART)
        return pltpu.make_async_copy(movie_hbm.at[span], movie.at[span], movie_sem.at[number])

    for number in range(BLK // PART):
        movie_part(number).start()
    send[...] = jnp.zeros_like(send)
    projected[...] = jnp.zeros_like(projected)
    foot_sorted[ENT:, :] = jnp.zeros((WINDOW, VOX), F32)
    block_sorted[ENT:, :] = jnp.full((WINDOW, 128), -1.0, F32)
    for copy in small[:3]:
        copy.wait()
    blk, own, slt = index[0], index[1], index[2]
    entry = iota((8, 128), 0) * 128 + iota((8, 128), 1)
    key = (blk * ENT + entry).astype(F32)
    ownf = own.astype(F32)
    key_col, own_col, blk_col = key.T, ownf.T, blk.astype(F32).T
    before = iota((128, 128), 0) < iota((128, 128), 1)
    lane8 = (iota((128, 128), 1) * 8).astype(F32)
    owner_rank, block_rank = [], []
    less = jnp.zeros((128, 128), F32)
    for row in range(8):
        key_row, own_row = key[row : row + 1, :], ownf[row : row + 1, :]
        count_o = jnp.zeros((128, 128), F32)
        count_k = jnp.zeros((128, 128), F32)
        for col in range(8):
            count_k += jnp.where(key_col[:, col : col + 1] < key_row, 1.0, 0.0)
            if col <= row:
                same = own_col[:, col : col + 1] == own_row
                if col == row:
                    same = same & before
                count_o += jnp.where(same, 1.0, 0.0)
        owner_rank.append(jnp.sum(count_o, axis=0, keepdims=True))
        block_rank.append(jnp.sum(count_k, axis=0, keepdims=True))
        less += jnp.where(blk_col[:, row : row + 1] < lane8, 1.0, 0.0)
    rank = jnp.concatenate(owner_rank, axis=0).astype(jnp.int32)
    order = jnp.concatenate(block_rank, axis=0).astype(jnp.int32)
    core, far, near = (own >> 2) & 1, own >> 3, own & 3
    message = jnp.where(core == 0, far, 4 + near)
    member = jnp.where(core == 0, near, far)
    tile, z = lax.axis_index("tile"), lax.axis_index("plane")
    turned = (member - jnp.where(core == 0, z, tile // 2) + 4) & 3
    section = jnp.where(turned == 0, 3, jnp.where(turned == 2, 0, jnp.where(turned == 1, 1, 2)))
    numbers[0] = message * ROWS + 8 + section * CAP + rank
    numbers[1] = order
    numbers[2] = jnp.broadcast_to(jnp.sum(less, axis=0, keepdims=True), (8, 128)).astype(jnp.int32)
    to_smem = pltpu.make_async_copy(numbers, numbers_s, sem.at[4])
    to_smem.start()

    small[3].wait()
    foot_values = foot[...].astype(F32)
    sq_high, sq_low = split(foot_values * foot_values)
    ones = jnp.ones((8, 128), BF16)
    energy = lax.dot_general(ones, sq_high, NT, preferred_element_type=F32) + lax.dot_general(
        ones, sq_low, NT, preferred_element_type=F32
    )
    place = section * 128 + rank
    meta = jnp.zeros((24, 512), F32)
    sorted_wide = jnp.zeros((ENT, 256), F32)
    for row in range(8):
        lanes = slice(row * 128, row * 128 + 128)
        chosen = message[row : row + 1, :] == iota((8, 128), 0)
        en_high, en_low = split(energy[:, lanes])
        slots = (slt[row : row + 1, :] + 1).astype(F32)
        values = jnp.concatenate(
            [
                jnp.where(chosen, slots, 0.0),
                jnp.where(chosen, en_high.astype(F32), 0.0),
                jnp.where(chosen, en_low.astype(F32), 0.0),
            ],
            axis=0,
        ).astype(BF16)
        places = jnp.where(place[row : row + 1, :] == iota((512, 128), 0), 1.0, 0.0).astype(BF16)
        meta += lax.dot_general(values, places, NT, preferred_element_type=F32)
        permute = jnp.where(order[row : row + 1, :] == iota((ENT, 128), 0), 1.0, 0.0).astype(BF16)
        wide = jnp.concatenate(
            [
                foot[lanes, :],
                jnp.broadcast_to(blk_col[:, row : row + 1], (128, 128)).astype(BF16),
            ],
            axis=1,
        )
        sorted_wide += jnp.dot(permute, wide, preferred_element_type=F32)
    foot_sorted[:ENT, :] = sorted_wide[:, :128]
    block_sorted[:ENT, :] = sorted_wide[:, 128:]
    for m in range(8):
        for i in range(4):
            lanes = slice(i * 128, i * 128 + 128)
            base = m * ROWS
            send[base + i : base + i + 1, :] = meta[m : m + 1, lanes]
            send[base + 4 + i : base + 5 + i, :] = (
                meta[8 + m : 9 + m, lanes] + meta[16 + m : 17 + m, lanes]
            )
    to_smem.wait()

    def product(chunk, first):
        span = pl.ds(pl.multiple_of(first, 8), WINDOW)
        values, which = foot_sorted[span, :], block_sorted[span, :]
        left = jnp.concatenate(
            [
                jnp.where(which == (chunk * 8 + n).astype(F32), values, 0.0).astype(BF16)
                for n in range(8)
            ],
            axis=1,
        )
        right = movie[pl.ds(chunk * 8, 8)].reshape(8 * VOX, FR)
        projected[span, :] += jnp.dot(left, right, preferred_element_type=F32)

    @pl.loop(0, BLK // PART)
    def _(group):
        movie_part(group).wait()
        windows(numbers_s, group, product)

    @pl.loop(0, 8)
    def _(line):
        for lane in range(128):
            send[pl.ds(numbers_s[0, line, lane], 1), :] = projected[
                pl.ds(numbers_s[1, line, lane], 1), :
            ]


def windows(numbers, group, product):
    count = PART // 8
    fits = None
    for k in range(count):
        chunk = group * count + k
        begin = (numbers[2, 0, chunk] // 8) * 8
        inside = numbers[2, 0, chunk + 1] - begin <= WINDOW
        fits = inside if fits is None else fits & inside

    @pl.when(fits)
    def _():
        for k in range(count):
            chunk = group * count + k
            product(chunk, (numbers[2, 0, chunk] // 8) * 8)

    @pl.when(jnp.logical_not(fits))
    def _():
        @pl.loop(0, count)
        def _(k):
            chunk = group * count + k
            begin = (numbers[2, 0, chunk] // 8) * 8
            number = jnp.maximum(1, (numbers[2, 0, chunk + 1] - begin + WINDOW - 1) // WINDOW)

            @pl.loop(0, number)
            def _(step):
                product(chunk, begin + step * WINDOW)


def gather(movie, footprint, entry_block, entry_owner, entry_slot):
    shape = jax.ShapeDtypeStruct
    in_place = pl.BlockSpec(memory_space=pltpu.HBM)
    return pl.pallas_call(
        gather_kernel,
        out_shape=(
            shape((8 * ROWS, FR), F32),
            shape((3, 8, 128), jnp.int32),
            shape((ENT + WINDOW, VOX), F32),
            shape((ENT + WINDOW, 128), F32),
        ),
        in_specs=[in_place] * 5,
        out_specs=(VMEM,) * 4,
        scratch_shapes=[
            pltpu.VMEM((BLK, VOX, FR), BF16),
            pltpu.VMEM((ENT, VOX), BF16),
            pltpu.VMEM((3, 8, 128), jnp.int32),
            pltpu.VMEM((ENT + WINDOW, FR), F32),
            pltpu.SMEM((3, 8, 128), jnp.int32),
            pltpu.SemaphoreType.DMA((5,)),
            pltpu.SemaphoreType.DMA((BLK // PART,)),
        ],
        compiler_params=pltpu.CompilerParams(vmem_limit_bytes=48 << 20),
        name="project",
    )(
        *(
            pltpu.with_memory_space_constraint(array, pltpu.HBM)
            for array in (
                movie, footprint, entry_block.reshape(8, 128),
                entry_owner.reshape(8, 128), entry_slot.reshape(8, 128),
            )
        )
    )


def pick(rows, sub):
    chosen = jnp.where(sub // 2 == 0, rows[0:1, :], rows[1:2, :])
    lane = iota((SUB, 128), 1) - lax.rem(sub, 2) * SUB
    return jnp.sum(jnp.where(lane == iota((SUB, 128), 0), chosen, 0.0), axis=1, keepdims=True)


def delayed(parts, steps):
    if steps >= 128:
        hop = steps // 128
        return [None] * hop + parts[: len(parts) - hop]
    lane = iota((SUB, 128), 1)
    rolled = [pltpu.roll(part, steps, 1) for part in parts]
    out = [jnp.where(lane < steps, 0.0, rolled[0])]
    for index in range(1, len(parts)):
        out.append(jnp.where(lane < steps, rolled[index - 1], rolled[index]))
    return out


def first_order(parts, powers):
    for level, power in enumerate(powers):
        moved = delayed(parts, 1 << level)
        parts = [
            part if late is None else part + power * late for part, late in zip(parts, moved)
        ]
    return parts


def sweeps(target, slow, fast):
    lag_one, lag_two = slow + fast, -slow * fast
    slow_powers, fast_powers = [slow], [fast]
    for _ in range(8):
        slow_powers.append(slow_powers[-1] * slow_powers[-1])
        fast_powers.append(fast_powers[-1] * fast_powers[-1])
    slow_share = slow / (slow - fast)
    fast_share = fast / (slow - fast)
    estimate = target
    for sweep in range(SWEEPS):
        one, two = delayed(estimate, 1), delayed(estimate, 2)
        spikes = [
            jnp.maximum(now - lag_one * a - lag_two * b, 0.0)
            for now, a, b in zip(estimate, one, two)
        ]
        slow_part = first_order(spikes, slow_powers)
        fast_part = first_order(spikes, fast_powers)
        calcium = [slow_share * a - fast_share * b for a, b in zip(slow_part, fast_part)]
        if sweep + 1 < SWEEPS:
            estimate = [0.5 * (a + b) for a, b in zip(target, calcium)]
    return calcium


def exchange_kernel(
    send, traces, slow, fast, back, calcium,
    got, hot, part, parts, piece, whole, reply,
    s1, r1, s2, r2, s3, r3, s4, r4, local,
):
    tile, y, z = lax.axis_index("tile"), lax.axis_index("tm"), lax.axis_index("plane")
    x, c = tile // 2, lax.rem(tile, 2)
    d = 1 - c
    p = x * d + z * c
    q = z * d + x * c

    def turn(value, by):
        return lax.rem(value + by, 4)

    def mine(pos, core):
        return (d * (2 * pos + core) + c * (2 * x + core), y, d * z + c * pos)

    def other(pos):
        return (c * 2 * pos + d * (2 * x + 1), y, c * z + d * pos)

    def column(pos, frame):
        return (d * 2 * x + c * (2 * pos + 1), frame, d * pos + c * z)

    reach = TURNS[:3]
    barrier = pltpu.get_barrier_semaphore()
    met = [mine(turn(p, by), c) for by in reach]
    met += [mine(turn(p, by), d) for by in TURNS]
    met += [other(turn(q, by)) for by in reach]
    met += [column(turn(q, dq), turn(y, dy)) for dq in TURNS for dy in TURNS if dq or dy]
    for device in met:
        pl.semaphore_signal(barrier, inc=1, device_id=device, device_id_type=MESH)
    pl.semaphore_wait(barrier, len(met))

    def remote(source, target, sends, arrives, device):
        return pltpu.make_async_remote_copy(
            src_ref=source, dst_ref=target, send_sem=sends, recv_sem=arrives,
            device_id=device, device_id_type=MESH,
        )

    def rows_of(section):
        return (0, 8 + CAP) if section == 0 else (8 + CAP * section, CAP)

    def message(index, section):
        first, count = rows_of(section)
        return send.at[pl.ds(pl.multiple_of(index * ROWS + first, 8), count), :]

    def landing(index, section):
        first, count = rows_of(section)
        return got.at[index, pl.ds(first, count), :]

    started = []

    def start(copy):
        copy.start()
        started.append(copy)

    own = pltpu.make_async_copy(
        send.at[pl.ds(pl.multiple_of((c * 4 + p) * ROWS, 8), ROWS), :], got.at[p * 2 + c], local.at[0]
    )
    own.start()
    for section in range(4):
        for by in TURNS:
            if by:
                index = c * 4 + turn(p, by)
                start(
                    remote(
                        message(index, section), landing(p * 2 + c, section),
                        s1.at[index * 4 + section], r1.at[(p * 2 + c) * 4 + section],
                        mine(turn(p, by), c),
                    )
                )
            index = d * 4 + turn(q, by)
            start(
                remote(
                    message(index, section), landing(q * 2 + c, section),
                    s1.at[index * 4 + section], r1.at[(q * 2 + c) * 4 + section],
                    other(turn(q, by)),
                )
            )

    slots_iota = (iota((OWN, 128), 0) + 1).astype(F32)
    ones = jnp.ones((8, 128), BF16)
    blank = jnp.zeros((128 - CAP, FR), BF16)
    top = iota((8, 128), 0) == 0
    sources = [(0, 0), (0, 1), (1, 0), (1, 1), (3, 0), (3, 1), (2, 0), (2, 1)]
    own.wait()
    for section in range(4):
        total = jnp.zeros((OWN, FR), F32)
        weight = jnp.zeros((OWN, 128), F32)
        first = 8 + CAP * section
        for by, flip in sources:
            source = turn(p, by) * 2 + (d if flip else c)
            if by or flip:
                remote(
                    message(0, section), landing(source, section), s1.at[0],
                    r1.at[source * 4 + section], mine(turn(p, by), c),
                ).wait_recv()
            match = slots_iota == got[source, section : section + 1, :]
            chosen = jnp.where(match, 1.0, 0.0).astype(BF16)
            hot[source, section] = chosen
            weight = weight + jnp.where(match, got[source, 4 + section : 5 + section, :], 0.0)
            high, low = split(got[source, first : first + CAP, :])
            total = total + jnp.dot(
                jnp.concatenate([chosen, chosen], axis=1),
                jnp.concatenate([high, blank, low, blank], axis=0),
                preferred_element_type=F32,
            )
        if section == 3:
            total = total + traces[...]
        high, low = split(weight)
        energy = lax.dot_general(ones, high, NT, preferred_element_type=F32) + lax.dot_general(
            ones, low, NT, preferred_element_type=F32
        )
        energy = jnp.where(top, energy[:, :128], energy[:, 128:])
        for sub in range(4):
            part[section, sub, :SUB, :] = total[sub * SUB : (sub + 1) * SUB, :]
            part[section, sub, SUB:, :] = energy
        tq = turn(q, TURNS[section])
        for dy in TURNS:
            ty = turn(y, dy)
            if section == 3 and dy == 0:
                own = pltpu.make_async_copy(part.at[section, y], parts.at[q, y], local.at[1])
                own.start()
            else:
                start(
                    remote(
                        part.at[section, ty], parts.at[q, y], s2.at[section * 4 + dy],
                        r2.at[q * 4 + y], column(tq, ty),
                    )
                )
    own.wait()
    for dq in TURNS:
        for dy in TURNS:
            if dq or dy:
                fq, fy = turn(q, dq), turn(y, dy)
                remote(
                    part.at[0, 0], parts.at[fq, fy], s2.at[0], r2.at[fq * 4 + fy], column(fq, fy)
                ).wait_recv()
    energy = parts[0, 0, SUB : SUB + 2, :]
    for other_q in range(1, 4):
        energy = energy + parts[other_q, 0, SUB : SUB + 2, :]
    scale = pick(energy, y) + 1.0
    target = []
    for frame in range(4):
        total = parts[0, frame, :SUB, :]
        for other_q in range(1, 4):
            total = total + parts[other_q, frame, :SUB, :]
        target.append(total / scale)
    traced = sweeps(target, pick(slow[...], y), pick(fast[...], y))
    for frame in range(4):
        piece[frame] = traced[frame]

    for section in (3, 1, 2, 0):
        tq = turn(q, TURNS[section])
        for dy in TURNS:
            ty = turn(y, dy)
            if section == 3 and dy == 0:
                own = pltpu.make_async_copy(piece.at[y], whole.at[q, y], local.at[2])
                own.start()
            else:
                start(
                    remote(
                        piece.at[ty], whole.at[q, y], s3.at[section * 4 + dy], r3.at[q * 4 + y],
                        column(tq, ty),
                    )
                )
    own.wait()

    def answer(index, section):
        return back.at[pl.ds(pl.multiple_of(index * ROWS + 8 + CAP * section, 8), CAP), :]

    for section in (3, 1, 2, 0):
        fq = turn(q, TURNS[section])
        for dy in TURNS:
            if section != 3 or dy:
                fy = turn(y, dy)
                remote(
                    piece.at[0], whole.at[fq, fy], s3.at[0], r3.at[fq * 4 + fy], column(fq, fy)
                ).wait_recv()
        if section == 3:
            for sub in range(4):
                calcium[sub * SUB : (sub + 1) * SUB, :] = whole[q, sub]
        rows = whole[fq].reshape(OWN, FR).astype(BF16)
        for order, (by, flip) in enumerate(sources[::-1]):
            core = d if flip else c
            source = turn(p, by) * 2 + core
            picked = lax.dot_general(hot[source, section], rows, TN, preferred_element_type=F32)
            reply[source, section] = picked[:CAP, :]
            if by or flip:
                start(
                    remote(
                        reply.at[source, section], answer(c * 4 + p, section),
                        s4.at[order * 4 + section], r4.at[(c * 4 + p) * 4 + section],
                        mine(turn(p, by), core),
                    )
                )
            else:
                own = pltpu.make_async_copy(
                    reply.at[source, section], answer(c * 4 + p, section), local.at[3 + section]
                )
                own.start()
                started.append(own)
    for section in (3, 1, 2, 0):
        for by in TURNS[::-1]:
            for core, pos in ((d, turn(q, by)), (c, turn(p, by))):
                if by == 0 and core is c:
                    continue
                index = core * 4 + pos
                remote(
                    reply.at[0, 0], answer(index, section), s4.at[0], r4.at[index * 4 + section],
                    other(q),
                ).wait_recv()
    for copy in started:
        if copy.is_remote:
            copy.wait_send()
        else:
            copy.wait()


def exchange(send, traces, slow_root, fast_root):
    dma = pltpu.SemaphoreType.DMA
    return pl.pallas_call(
        exchange_kernel,
        out_shape=(
            jax.ShapeDtypeStruct((8 * ROWS, FR), F32),
            jax.ShapeDtypeStruct((OWN, FR), F32),
        ),
        in_specs=[VMEM] * 4,
        out_specs=(VMEM, VMEM),
        scratch_shapes=[
            pltpu.VMEM((8, ROWS, FR), F32),
            pltpu.VMEM((8, 4, OWN, 128), BF16),
            pltpu.VMEM((4, 4, PIECE, FR), F32),
            pltpu.VMEM((4, 4, PIECE, FR), F32),
            pltpu.VMEM((4, SUB, FR), F32),
            pltpu.VMEM((4, 4, SUB, FR), F32),
            pltpu.VMEM((8, 4, CAP, FR), F32),
            dma((32,)), dma((32,)), dma((16,)), dma((16,)),
            dma((16,)), dma((16,)), dma((32,)), dma((32,)), dma((7,)),
        ],
        compiler_params=pltpu.CompilerParams(
            collective_id=1, has_side_effects=True, vmem_limit_bytes=48 << 20
        ),
        name="exchange",
    )(send, traces, slow_root.reshape(2, 128), fast_root.reshape(2, 128))


def rebuild_kernel(
    numbers_v, back, foot, block, calcium, out_hbm, calcium_out, numbers, rows, out, total, sem
):
    to_smem = pltpu.make_async_copy(numbers_v, numbers, sem.at[BLK // PART])
    to_smem.start()
    calcium_out[...] = calcium[...]
    rows[ENT:, :] = jnp.zeros((WINDOW, FR), F32)
    to_smem.wait()

    @pl.loop(0, 8)
    def _(line):
        for lane in range(128):
            rows[pl.ds(numbers[1, line, lane], 1), :] = back[
                pl.ds(numbers[0, line, lane], 1), :
            ]

    def product(chunk, first):
        span = pl.ds(pl.multiple_of(first, 8), WINDOW)
        values, which = rows[span, :], block[span, :]
        masked = jnp.concatenate(
            [
                jnp.where(which == (chunk * 8 + n).astype(F32), values, 0.0).astype(BF16)
                for n in range(8)
            ],
            axis=1,
        )
        left = foot[span, :].astype(BF16)
        return lax.dot_general(left, masked, TN, preferred_element_type=F32)

    def out_part(number):
        span = pl.ds(number * PART, PART)
        return pltpu.make_async_copy(out.at[span], out_hbm.at[span], sem.at[number])

    def store(chunk, result):
        for n in range(8):
            out[chunk * 8 + n] = result[:, n * FR : (n + 1) * FR].astype(BF16)

    count = PART // 8

    @pl.loop(0, BLK // PART)
    def _(group):
        fits = None
        for k in range(count):
            chunk = group * count + k
            inside = numbers[2, 0, chunk + 1] - (numbers[2, 0, chunk] // 8) * 8 <= WINDOW
            fits = inside if fits is None else fits & inside

        @pl.when(fits)
        def _():
            for k in range(count):
                chunk = group * count + k
                store(chunk, product(chunk, (numbers[2, 0, chunk] // 8) * 8))

        @pl.when(jnp.logical_not(fits))
        def _():
            @pl.loop(0, count)
            def _(k):
                chunk = group * count + k
                begin = (numbers[2, 0, chunk] // 8) * 8
                number = jnp.maximum(1, (numbers[2, 0, chunk + 1] - begin + WINDOW - 1) // WINDOW)
                total[...] = product(chunk, begin)

                @pl.loop(1, number)
                def _(step):
                    total[...] += product(chunk, begin + step * WINDOW)

                store(chunk, total[...])

        out_part(group).start()

    @pl.loop(0, BLK // PART)
    def _(group):
        out_part(group).wait()


def rebuild(numbers, back, foot, block, calcium):
    return pl.pallas_call(
        rebuild_kernel,
        out_shape=(
            jax.ShapeDtypeStruct((BLK, VOX, FR), BF16),
            jax.ShapeDtypeStruct((OWN, FR), F32),
        ),
        in_specs=[VMEM] * 5,
        out_specs=(pl.BlockSpec(memory_space=pl.ANY), VMEM),
        scratch_shapes=[
            pltpu.SMEM((3, 8, 128), jnp.int32),
            pltpu.VMEM((ENT + WINDOW, FR), F32),
            pltpu.VMEM((BLK, VOX, FR), BF16),
            pltpu.VMEM((VOX, 8 * FR), F32),
            pltpu.SemaphoreType.DMA((BLK // PART + 1,)),
        ],
        compiler_params=pltpu.CompilerParams(vmem_limit_bytes=48 << 20),
        name="rebuild",
    )(numbers, back, foot, block, calcium)


def shards(movie, footprint, entry_block, entry_owner, entry_slot, traces, slow_root, fast_root):
    send, numbers, foot, block = gather(
        movie, footprint, entry_block, entry_owner, entry_slot
    )
    back, calcium = exchange(send, traces, slow_root, fast_root)
    return rebuild(numbers, back, foot, block, calcium)


def solution(mesh):
    owners = ("tile", "plane")
    placed = (
        P(owners, None, "tm"),
        P(owners, None),
        P(owners),
        P(owners, None),
        P(owners),
        P(owners, "tm"),
        P(owners),
        P(owners),
    )
    return jax.shard_map(
        shards,
        mesh=mesh,
        in_specs=placed,
        out_specs=(P(owners, None, "tm"), P(owners, "tm")),
        check_vma=False,
    )
```

time: 75.2 us -> 64 us (0.85)
  Pallas kernels: 68.6 us -> 63 us
  local copies, waits for them, and re-layouts: 5.57 us -> 0.01 us
    unnamed x18 -> x6, local copies, waits for them, and re-layouts: 5.57 us -> 0.01 us
    pallas_call x1, Pallas kernels: 50.8 us -> 46.7 us  [exchange(): pl.pallas_call(exchange_kernel, out_shape=(jax.ShapeDtypeStruct((8 * ROWS...]
    pallas_call x1, Pallas kernels: 10.5 us -> 8.63 us  [gather(): pl.pallas_call(gather_kernel, out_shape=(shape((8 * ROWS, FR), F32), shap...]
where the time goes in v3:
time: 64 us; the launch traced here: 63.7 us
  Pallas kernels  63 us (98%)
  between operations  0.7 us (1%)
    pallas_call x1, Pallas kernels, exchange(): pl.pallas_call(exchange_kernel, out_shape=(jax.ShapeDtypeStruct((8 * ROWS...  46.7 us
    pallas_call x1, Pallas kernels, gather(): pl.pallas_call(gather_kernel, out_shape=(shape((8 * ROWS, FR), F32), shap...  8.63 us
    pallas_call x1, Pallas kernels, rebuild(): pl.pallas_call(rebuild_kernel, out_shape=(jax.ShapeDtypeStruct((BLK, VOX,...  7.66 us

profile of v3, /device:TPU:0, one launch (start us, length us, event | category | flops | bytes accessed | tf_op | source)
XLA Modules:
  0.0 63.7 jit_solution(535060838514775719)
XLA Ops:
  0.6 0.0 copy-start.2
  0.6 0.0 copy-start.1
  0.7 0.0 copy-start
  0.7 8.6 %project.1 = (f32[3136,128]{1,0:T(8,128)S(1)}, s32[3,8,128]{2,1,0:T(8,128)S(1)}, f32[1088,128]{1,0:T(8,128)S(1)}, f32[1088,128]{1,0:T(8,128)S(1)}) custom-call(bf16[256,128,128]{2,1,0:T(8,128)(2,1)} %movie_hbm.1, bf16[1024,128]{1,0:T(8,128)(2,1)} %foot_hbm.1, s32[8,128]{1,0:T(8,128)} %bitcast.7, s32[8,128]{1,0:T(8,128)} %bitcast.8, s32[8,128]{1,0:T(8,128)} %bitcast.9), custom_call_target="tpu_custom_call" | custom-call | tf_op jit(solution)/shard_map/project/pallas_call | solution.py:205
  9.3 0.0 copy-done.2
  9.3 0.0 copy-done.1
  9.3 0.0 copy-done
  9.3 46.7 %exchange.1 = (f32[3136,128]{1,0:T(8,128)S(1)}, f32[256,128]{1,0:T(8,128)S(1)}) custom-call(f32[3136,128]{1,0:T(8,128)S(1)} %get-tuple-element.9.send, f32[256,128]{1,0:T(8,128)S(1)} %copy-done, f32[2,128]{1,0:T(2,128)S(1)} %bitcast.5, f32[2,128]{1,0:T(2,128)S(1)} %bitcast.6), custom_call_target="tpu_custom_call" | custom-call | tf_op jit(solution)/shard_map/exchange/pallas_call | solution.py:508
  56.0 7.7 %rebuild.1 = (bf16[256,128,128]{2,1,0:T(8,128)(2,1)}, f32[256,128]{1,0:T(8,128)}) custom-call(s32[3,8,128]{2,1,0:T(8,128)S(1)} %get-tuple-element.8.numbers_v, f32[3136,128]{1,0:T(8,128)S(1)} %get-tuple-element.10.back, f32[1088,128]{1,0:T(8,128)S(1)} %get-tuple-element.11.foot, f32[1088,128]{1,0:T(8,128)S(1)} %get-tuple-element.12.block, ...), custom_call_target="tpu_custom_call" | custom-call | tf_op jit(solution)/shard_map/rebuild/pallas_call | solution.py:610
Async XLA Ops:
  0.6 8.7 %copy-start.2 = (f32[256]{0:T(256)S(1)}, f32[256]{0:T(256)}, u32[]{:S(2)}) copy-start(f32[256]{0:T(256)} %param.15) | copy-start | bytes 3076
  0.6 8.7 %copy-start.1 = (f32[256]{0:T(256)S(1)}, f32[256]{0:T(256)}, u32[]{:S(2)}) copy-start(f32[256]{0:T(256)} %param.14) | copy-start | bytes 3076
  0.7 8.7 %copy-start = (f32[256,128]{1,0:T(8,128)S(1)}, f32[256,128]{1,0:T(8,128)}, u32[]{:S(2)}) copy-start(f32[256,128]{1,0:T(8,128)} %traces.1) | copy-start | bytes 393220

commit v4 on v3

--- a/solution.py
+++ b/solution.py
@@ -38,8 +38,8 @@
 
 def gather_kernel(
     movie_hbm, foot_hbm, block_hbm, owner_hbm, slot_hbm,
-    send, numbers, foot_sorted, block_sorted,
-    movie, foot, index, projected, numbers_s, sem, movie_sem,
+    projected, labels, inverse, numbers, foot_sorted, block_sorted,
+    movie, foot, index, numbers_s, sem, movie_sem,
 ):
     small = [
         pltpu.make_async_copy(source, target, sem.at[number])
@@ -56,7 +56,6 @@
 
     for number in range(BLK // PART):
         movie_part(number).start()
-    send[...] = jnp.zeros_like(send)
     projected[...] = jnp.zeros_like(projected)
     foot_sorted[ENT:, :] = jnp.zeros((WINDOW, VOX), F32)
     block_sorted[ENT:, :] = jnp.full((WINDOW, 128), -1.0, F32)
@@ -107,18 +106,21 @@
         ones, sq_low, NT, preferred_element_type=F32
     )
     place = section * 128 + rank
-    meta = jnp.zeros((24, 512), F32)
+    meta = jnp.zeros((40, 512), F32)
     sorted_wide = jnp.zeros((ENT, 256), F32)
     for row in range(8):
         lanes = slice(row * 128, row * 128 + 128)
         chosen = message[row : row + 1, :] == iota((8, 128), 0)
         en_high, en_low = split(energy[:, lanes])
         slots = (slt[row : row + 1, :] + 1).astype(F32)
+        sorted_at = order[row : row + 1, :] + 1
         values = jnp.concatenate(
             [
                 jnp.where(chosen, slots, 0.0),
                 jnp.where(chosen, en_high.astype(F32), 0.0),
                 jnp.where(chosen, en_low.astype(F32), 0.0),
+                jnp.where(chosen, (sorted_at >> 5).astype(F32), 0.0),
+                jnp.where(chosen, (sorted_at & 31).astype(F32), 0.0),
             ],
             axis=0,
         ).astype(BF16)
@@ -135,14 +137,14 @@
         sorted_wide += jnp.dot(permute, wide, preferred_element_type=F32)
     foot_sorted[:ENT, :] = sorted_wide[:, :128]
     block_sorted[:ENT, :] = sorted_wide[:, 128:]
-    for m in range(8):
-        for i in range(4):
-            lanes = slice(i * 128, i * 128 + 128)
-            base = m * ROWS
-            send[base + i : base + i + 1, :] = meta[m : m + 1, lanes]
-            send[base + 4 + i : base + 5 + i, :] = (
-                meta[8 + m : 9 + m, lanes] + meta[16 + m : 17 + m, lanes]
-            )
+    place_of = (meta[24:32, :] * 32.0 + meta[32:40, :]).astype(jnp.int32)
+    place_of = jnp.where(place_of == 0, ENT, place_of - 1)
+    weights = meta[8:16, :] + meta[16:24, :]
+    for i in range(4):
+        lanes = slice(i * 128, i * 128 + 128)
+        inverse[i] = place_of[:, lanes]
+        labels[:, i, :] = meta[:8, lanes]
+        labels[:, 4 + i, :] = weights[:, lanes]
     to_smem.wait()
 
     def product(chunk, first):
@@ -163,13 +165,6 @@
         movie_part(group).wait()
         windows(numbers_s, group, product)
 
-    @pl.loop(0, 8)
-    def _(line):
-        for lane in range(128):
-            send[pl.ds(numbers_s[0, line, lane], 1), :] = projected[
-                pl.ds(numbers_s[1, line, lane], 1), :
-            ]
-
 
 def windows(numbers, group, product):
     count = PART // 8
@@ -205,18 +200,19 @@
     return pl.pallas_call(
         gather_kernel,
         out_shape=(
-            shape((8 * ROWS, FR), F32),
+            shape((ENT + WINDOW, FR), F32),
+            shape((8, 8, 128), F32),
+            shape((4, 8, 128), jnp.int32),
             shape((3, 8, 128), jnp.int32),
             shape((ENT + WINDOW, VOX), F32),
             shape((ENT + WINDOW, 128), F32),
         ),
         in_specs=[in_place] * 5,
-        out_specs=(VMEM,) * 4,
+        out_specs=(VMEM,) * 6,
         scratch_shapes=[
             pltpu.VMEM((BLK, VOX, FR), BF16),
             pltpu.VMEM((ENT, VOX), BF16),
             pltpu.VMEM((3, 8, 128), jnp.int32),
-            pltpu.VMEM((ENT + WINDOW, FR), F32),
             pltpu.SMEM((3, 8, 128), jnp.int32),
             pltpu.SemaphoreType.DMA((5,)),
             pltpu.SemaphoreType.DMA((BLK // PART,)),
@@ -285,8 +281,8 @@
 
 
 def exchange_kernel(
-    send, traces, slow, fast, back, calcium,
-    got, hot, part, parts, piece, whole, reply,
+    projected, labels, inverse_v, traces, slow, fast, back, calcium,
+    inverse, send, got, hot, part, parts, piece, whole, reply,
     s1, r1, s2, r2, s3, r3, s4, r4, local,
 ):
     tile, y, z = lax.axis_index("tile"), lax.axis_index("tm"), lax.axis_index("plane")
@@ -307,6 +303,8 @@
     def column(pos, frame):
         return (d * 2 * x + c * (2 * pos + 1), frame, d * pos + c * z)
 
+    to_smem = pltpu.make_async_copy(inverse_v, inverse, local.at[0])
+    to_smem.start()
     reach = TURNS[:3]
     barrier = pltpu.get_barrier_semaphore()
     met = [mine(turn(p, by), c) for by in reach]
@@ -315,6 +313,21 @@
     met += [column(turn(q, dq), turn(y, dy)) for dq in TURNS for dy in TURNS if dq or dy]
     for device in met:
         pl.semaphore_signal(barrier, inc=1, device_id=device, device_id_type=MESH)
+    for index in range(8):
+        send[index * ROWS : index * ROWS + 8, :] = labels[index]
+
+    def place(section):
+        @pl.loop(0, 8)
+        def _(index):
+            first = pl.multiple_of(index * ROWS + 8 + CAP * section, 8)
+            for block in range(0, CAP, 8):
+                rows = [
+                    projected[pl.ds(inverse[section, index, block + row], 1), :] for row in range(8)
+                ]
+                send[pl.ds(first + block, 8), :] = jnp.concatenate(rows, axis=0)
+
+    to_smem.wait()
+    place(0)
     pl.semaphore_wait(barrier, len(met))
 
     def remote(source, target, sends, arrives, device):
@@ -340,11 +353,7 @@
         copy.start()
         started.append(copy)
 
-    own = pltpu.make_async_copy(
-        send.at[pl.ds(pl.multiple_of((c * 4 + p) * ROWS, 8), ROWS), :], got.at[p * 2 + c], local.at[0]
-    )
-    own.start()
-    for section in range(4):
+    def send_section(section):
         for by in TURNS:
             if by:
                 index = c * 4 + turn(p, by)
@@ -364,33 +373,50 @@
                 )
             )
 
+    for section in range(4):
+        if section:
+            place(section)
+        send_section(section)
+
     slots_iota = (iota((OWN, 128), 0) + 1).astype(F32)
     ones = jnp.ones((8, 128), BF16)
     blank = jnp.zeros((128 - CAP, FR), BF16)
     top = iota((8, 128), 0) == 0
     sources = [(0, 0), (0, 1), (1, 0), (1, 1), (3, 0), (3, 1), (2, 0), (2, 1)]
-    own.wait()
     for section in range(4):
-        total = jnp.zeros((OWN, FR), F32)
         weight = jnp.zeros((OWN, 128), F32)
+        lefts, rights = [], []
         first = 8 + CAP * section
-        for by, flip in sources:
+        for by, flip in sources[1:]:
             source = turn(p, by) * 2 + (d if flip else c)
+            remote(
+                message(0, section), landing(source, section), s1.at[0],
+                r1.at[source * 4 + section], mine(turn(p, by), c),
+            ).wait_recv()
+        for place_in, (by, flip) in enumerate(sources):
             if by or flip:
-                remote(
-                    message(0, section), landing(source, section), s1.at[0],
-                    r1.at[source * 4 + section], mine(turn(p, by), c),
-                ).wait_recv()
-            match = slots_iota == got[source, section : section + 1, :]
-            chosen = jnp.where(match, 1.0, 0.0).astype(BF16)
-            hot[source, section] = chosen
-            weight = weight + jnp.where(match, got[source, 4 + section : 5 + section, :], 0.0)
-            high, low = split(got[source, first : first + CAP, :])
-            total = total + jnp.dot(
-                jnp.concatenate([chosen, chosen], axis=1),
-                jnp.concatenate([high, blank, low, blank], axis=0),
-                preferred_element_type=F32,
-            )
+                source = turn(p, by) * 2 + (d if flip else c)
+                slots = got[source, section : section + 1, :]
+                energies = got[source, 4 + section : 5 + section, :]
+                values = got[source, first : first + CAP, :]
+            else:
+                base = (c * 4 + p) * ROWS
+                slots = labels[c * 4 + p, section : section + 1, :]
+                energies = labels[c * 4 + p, 4 + section : 5 + section, :]
+                values = send[pl.ds(pl.multiple_of(base + first, 8), CAP), :]
+            match = slots_iota == slots
+            chosen = jnp.where(match, 1.0, 0.0)
+            hot[section, place_in * CAP : (place_in + 1) * CAP, :] = chosen.T[:CAP, :].astype(BF16)
+            weight = weight + jnp.where(match, energies, 0.0)
+            high, low = split(values)
+            chosen = chosen.astype(BF16)
+            lefts += [chosen, chosen]
+            rights += [high, blank, low, blank]
+        total = jnp.dot(
+            jnp.concatenate(lefts, axis=1),
+            jnp.concatenate(rights, axis=0),
+            preferred_element_type=F32,
+        )
         if section == 3:
             total = total + traces[...]
         high, low = split(weight)
@@ -408,10 +434,11 @@
                 own = pltpu.make_async_copy(part.at[section, y], parts.at[q, y], local.at[1])
                 own.start()
             else:
+                count = SUB if dy else PIECE
                 start(
                     remote(
-                        part.at[section, ty], parts.at[q, y], s2.at[section * 4 + dy],
-                        r2.at[q * 4 + y], column(tq, ty),
+                        part.at[section, ty, pl.ds(0, count)], parts.at[q, y, pl.ds(0, count)],
+                        s2.at[section * 4 + dy], r2.at[q * 4 + y], column(tq, ty),
                     )
                 )
     own.wait()
@@ -419,12 +446,14 @@
         for dy in TURNS:
             if dq or dy:
                 fq, fy = turn(q, dq), turn(y, dy)
+                count = SUB if dy else PIECE
                 remote(
-                    part.at[0, 0], parts.at[fq, fy], s2.at[0], r2.at[fq * 4 + fy], column(fq, fy)
+                    part.at[0, 0, pl.ds(0, count)], parts.at[fq, fy, pl.ds(0, count)], s2.at[0],
+                    r2.at[fq * 4 + fy], column(fq, fy),
                 ).wait_recv()
-    energy = parts[0, 0, SUB : SUB + 2, :]
+    energy = parts[0, y, SUB : SUB + 2, :]
     for other_q in range(1, 4):
-        energy = energy + parts[other_q, 0, SUB : SUB + 2, :]
+        energy = energy + parts[other_q, y, SUB : SUB + 2, :]
     scale = pick(energy, y) + 1.0
     target = []
     for frame in range(4):
@@ -467,22 +496,22 @@
             for sub in range(4):
                 calcium[sub * SUB : (sub + 1) * SUB, :] = whole[q, sub]
         rows = whole[fq].reshape(OWN, FR).astype(BF16)
-        for order, (by, flip) in enumerate(sources[::-1]):
+        reply[section] = jnp.dot(hot[section], rows, preferred_element_type=F32)
+        for order in range(7, -1, -1):
+            by, flip = sources[order]
             core = d if flip else c
-            source = turn(p, by) * 2 + core
-            picked = lax.dot_general(hot[source, section], rows, TN, preferred_element_type=F32)
-            reply[source, section] = picked[:CAP, :]
             if by or flip:
                 start(
                     remote(
-                        reply.at[source, section], answer(c * 4 + p, section),
+                        reply.at[section, pl.ds(order * CAP, CAP)], answer(c * 4 + p, section),
                         s4.at[order * 4 + section], r4.at[(c * 4 + p) * 4 + section],
                         mine(turn(p, by), core),
                     )
                 )
             else:
                 own = pltpu.make_async_copy(
-                    reply.at[source, section], answer(c * 4 + p, section), local.at[3 + section]
+                    reply.at[section, pl.ds(order * CAP, CAP)], answer(c * 4 + p, section),
+                    local.at[3 + section],
                 )
                 own.start()
                 started.append(own)
@@ -493,7 +522,7 @@
                     continue
                 index = core * 4 + pos
                 remote(
-                    reply.at[0, 0], answer(index, section), s4.at[0], r4.at[index * 4 + section],
+                    reply.at[0, pl.ds(0, CAP)], answer(index, section), s4.at[0], r4.at[index * 4 + section],
                     other(q),
                 ).wait_recv()
     for copy in started:
@@ -503,7 +532,7 @@
             copy.wait()
 
 
-def exchange(send, traces, slow_root, fast_root):
+def exchange(projected, labels, inverse, traces, slow_root, fast_root):
     dma = pltpu.SemaphoreType.DMA
     return pl.pallas_call(
         exchange_kernel,
@@ -511,16 +540,18 @@
             jax.ShapeDtypeStruct((8 * ROWS, FR), F32),
             jax.ShapeDtypeStruct((OWN, FR), F32),
         ),
-        in_specs=[VMEM] * 4,
+        in_specs=[VMEM] * 6,
         out_specs=(VMEM, VMEM),
         scratch_shapes=[
+            pltpu.SMEM((4, 8, 128), jnp.int32),
+            pltpu.VMEM((8 * ROWS, FR), F32),
             pltpu.VMEM((8, ROWS, FR), F32),
-            pltpu.VMEM((8, 4, OWN, 128), BF16),
+            pltpu.VMEM((4, 8 * CAP, OWN), BF16),
             pltpu.VMEM((4, 4, PIECE, FR), F32),
             pltpu.VMEM((4, 4, PIECE, FR), F32),
             pltpu.VMEM((4, SUB, FR), F32),
             pltpu.VMEM((4, 4, SUB, FR), F32),
-            pltpu.VMEM((8, 4, CAP, FR), F32),
+            pltpu.VMEM((4, 8 * CAP, FR), F32),
             dma((32,)), dma((32,)), dma((16,)), dma((16,)),
             dma((16,)), dma((16,)), dma((32,)), dma((32,)), dma((7,)),
         ],
@@ -528,7 +559,7 @@
             collective_id=1, has_side_effects=True, vmem_limit_bytes=48 << 20
         ),
         name="exchange",
-    )(send, traces, slow_root.reshape(2, 128), fast_root.reshape(2, 128))
+    )(projected, labels, inverse, traces, slow_root.reshape(2, 128), fast_root.reshape(2, 128))
 
 
 def rebuild_kernel(
@@ -628,10 +659,10 @@
 
 
 def shards(movie, footprint, entry_block, entry_owner, entry_slot, traces, slow_root, fast_root):
-    send, numbers, foot, block = gather(
+    projected, labels, inverse, numbers, foot, block = gather(
         movie, footprint, entry_block, entry_owner, entry_slot
     )
-    back, calcium = exchange(send, traces, slow_root, fast_root)
+    back, calcium = exchange(projected, labels, inverse, traces, slow_root, fast_root)
     return rebuild(numbers, back, foot, block, calcium)
 
 

time: 64 us -> 61.5 us (0.961)
  Pallas kernels: 63 us -> 60 us
    pallas_call x1, Pallas kernels: 8.63 us -> 7 us  [gather(): pl.pallas_call(gather_kernel, out_shape=(shape((ENT + WINDOW, FR), F32),...]
    pallas_call x1, Pallas kernels: 46.7 us -> 45.4 us  [exchange(): pl.pallas_call(exchange_kernel, out_shape=(jax.ShapeDtypeStruct((8 * ROWS...]
where the time goes in v4:
time: 61.5 us; the launch traced here: 60.7 us
  Pallas kernels  60 us (98%)
  between operations  0.7 us (1%)
    pallas_call x1, Pallas kernels, exchange(): pl.pallas_call(exchange_kernel, out_shape=(jax.ShapeDtypeStruct((8 * ROWS...  45.4 us
    pallas_call x1, Pallas kernels, rebuild(): pl.pallas_call(rebuild_kernel, out_shape=(jax.ShapeDtypeStruct((BLK, VOX,...  7.65 us
    pallas_call x1, Pallas kernels, gather(): pl.pallas_call(gather_kernel, out_shape=(shape((ENT + WINDOW, FR), F32),...  7 us

profile of v4, /device:TPU:0, one launch (start us, length us, event | category | flops | bytes accessed | tf_op | source)
XLA Modules:
  0.0 60.7 jit_solution(8902034430742673458)
XLA Ops:
  0.6 0.0 copy-start.2
  0.6 0.0 copy-start.1
  0.7 0.0 copy-start
  0.7 7.0 %project.1 = (f32[1088,128]{1,0:T(8,128)S(1)}, f32[8,8,128]{2,1,0:T(8,128)S(1)}, s32[4,8,128]{2,1,0:T(8,128)S(1)}, s32[3,8,128]{2,1,0:T(8,128)S(1)}, f32[1088,128]{1,0:T(8,128)S(1)}, /*index=5*/f32[1088,128]{1,0:T(8,128)S(1)}) custom-call(bf16[256,128,128]{2,1,0:T(8,128)(2,1)} %movie_hbm.1, bf16[1024,128]{1,0:T(8,128)(2,1)} %foot_hbm.1, s32[8,128]{1,0:T(8,128)} %bitcast.7, ...), custom_call_target="tpu_custom_call" | custom-call | tf_op jit(solution)/shard_map/project/pallas_call | solution.py:200
  7.7 0.0 copy-done.2
  7.7 0.0 copy-done.1
  7.7 0.0 copy-done
  7.7 45.4 %exchange.1 = (f32[3136,128]{1,0:T(8,128)S(1)}, f32[256,128]{1,0:T(8,128)S(1)}) custom-call(f32[1088,128]{1,0:T(8,128)S(1)} %get-tuple-element.11.projected, f32[8,8,128]{2,1,0:T(8,128)S(1)} %get-tuple-element.12.labels, s32[4,8,128]{2,1,0:T(8,128)S(1)} %get-tuple-element.13.inverse_v, f32[256,128]{1,0:T(8,128)S(1)} %copy-done, f32[2,128]{1,0:T(2,128)S(1)} %bitcast.5, ...), custom_call_target="tpu_custom_call" | custom-call | tf_op jit(solution)/shard_map/exchange/pallas_call | solution.py:537
  53.1 7.7 %rebuild.1 = (bf16[256,128,128]{2,1,0:T(8,128)(2,1)}, f32[256,128]{1,0:T(8,128)}) custom-call(s32[3,8,128]{2,1,0:T(8,128)S(1)} %get-tuple-element.10.numbers_v, f32[3136,128]{1,0:T(8,128)S(1)} %get-tuple-element.14.back, f32[1088,128]{1,0:T(8,128)S(1)} %get-tuple-element.15.foot, f32[1088,128]{1,0:T(8,128)S(1)} %get-tuple-element.16.block, ...), custom_call_target="tpu_custom_call" | custom-call | tf_op jit(solution)/shard_map/rebuild/pallas_call | solution.py:641
Async XLA Ops:
  0.6 7.0 %copy-start.2 = (f32[256]{0:T(256)S(1)}, f32[256]{0:T(256)}, u32[]{:S(2)}) copy-start(f32[256]{0:T(256)} %param.15) | copy-start | bytes 3076
  0.6 7.0 %copy-start.1 = (f32[256]{0:T(256)S(1)}, f32[256]{0:T(256)}, u32[]{:S(2)}) copy-start(f32[256]{0:T(256)} %param.14) | copy-start | bytes 3076
  0.7 7.0 %copy-start = (f32[256,128]{1,0:T(8,128)S(1)}, f32[256,128]{1,0:T(8,128)}, u32[]{:S(2)}) copy-start(f32[256,128]{1,0:T(8,128)} %traces.1) | copy-start | bytes 393220

commit v5 on v4

--- a/solution.py
+++ b/solution.py
@@ -18,7 +18,7 @@
 SUB = OWN // 4
 PIECE = SUB + 8
 WINDOW = 64
-PART = 64
+PART = 32
 MESH = pl.DeviceIdType.MESH
 F32 = jnp.float32
 BF16 = jnp.bfloat16
@@ -39,7 +39,7 @@
 def gather_kernel(
     movie_hbm, foot_hbm, block_hbm, owner_hbm, slot_hbm,
     projected, labels, inverse, numbers, foot_sorted, block_sorted,
-    movie, foot, index, numbers_s, sem, movie_sem,
+    movie, foot, index, numbers_s, sem,
 ):
     small = [
         pltpu.make_async_copy(source, target, sem.at[number])
@@ -50,12 +50,8 @@
     for copy in small:
         copy.start()
 
-    def movie_part(number):
-        span = pl.ds(number * PART, PART)
-        return pltpu.make_async_copy(movie_hbm.at[span], movie.at[span], movie_sem.at[number])
-
-    for number in range(BLK // PART):
-        movie_part(number).start()
+    load = pltpu.make_async_copy(movie_hbm, movie, sem.at[5])
+    load.start()
     projected[...] = jnp.zeros_like(projected)
     foot_sorted[ENT:, :] = jnp.zeros((WINDOW, VOX), F32)
     block_sorted[ENT:, :] = jnp.full((WINDOW, 128), -1.0, F32)
@@ -94,7 +90,13 @@
     section = jnp.where(turned == 0, 3, jnp.where(turned == 2, 0, jnp.where(turned == 1, 1, 2)))
     numbers[0] = message * ROWS + 8 + section * CAP + rank
     numbers[1] = order
-    numbers[2] = jnp.broadcast_to(jnp.sum(less, axis=0, keepdims=True), (8, 128)).astype(jnp.int32)
+    begins = jnp.broadcast_to(jnp.sum(less, axis=0, keepdims=True), (8, 128)).astype(jnp.int32)
+    beyond = pltpu.roll(begins, 127, 1) - (begins >> 3) * 8 > WINDOW
+    lane = iota((8, 128), 1)
+    misfits = jnp.sum(
+        jnp.where(beyond & (lane < BLK // 8), 1.0, 0.0), axis=1, keepdims=True
+    ).astype(jnp.int32)
+    numbers[2] = jnp.where(lane == 127, misfits, begins)
     to_smem = pltpu.make_async_copy(numbers, numbers_s, sem.at[4])
     to_smem.start()
 
@@ -147,51 +149,53 @@
         labels[:, 4 + i, :] = weights[:, lanes]
     to_smem.wait()
 
-    def product(chunk, first):
-        span = pl.ds(pl.multiple_of(first, 8), WINDOW)
-        values, which = foot_sorted[span, :], block_sorted[span, :]
-        left = jnp.concatenate(
-            [
-                jnp.where(which == (chunk * 8 + n).astype(F32), values, 0.0).astype(BF16)
-                for n in range(8)
-            ],
-            axis=1,
-        )
+    def product(chunk, begin, steps):
         right = movie[pl.ds(chunk * 8, 8)].reshape(8 * VOX, FR)
-        projected[span, :] += jnp.dot(left, right, preferred_element_type=F32)
-
-    @pl.loop(0, BLK // PART)
-    def _(group):
-        movie_part(group).wait()
-        windows(numbers_s, group, product)
-
-
-def windows(numbers, group, product):
+
+        def add(step):
+            span = pl.ds(pl.multiple_of(begin + step * WINDOW, 8), WINDOW)
+            values, which = foot_sorted[span, :], block_sorted[span, :]
+            left = jnp.concatenate(
+                [
+                    jnp.where(which == jnp.asarray(chunk * 8 + n, F32), values, 0.0).astype(BF16)
+                    for n in range(8)
+                ],
+                axis=1,
+            )
+            projected[span, :] += jnp.dot(left, right, preferred_element_type=F32)
+
+        if isinstance(steps, int):
+            add(0)
+        else:
+            pl.loop(0, steps)(add)
+
+    load.wait()
+    windows(numbers_s, product, lambda group: None)
+
+
+def windows(numbers, product, after):
     count = PART // 8
-    fits = None
-    for k in range(count):
-        chunk = group * count + k
-        begin = (numbers[2, 0, chunk] // 8) * 8
-        inside = numbers[2, 0, chunk + 1] - begin <= WINDOW
-        fits = inside if fits is None else fits & inside
-
-    @pl.when(fits)
+    misfits = numbers[2, 0, 127]
+
+    @pl.when(misfits == 0)
     def _():
-        for k in range(count):
-            chunk = group * count + k
-            product(chunk, (numbers[2, 0, chunk] // 8) * 8)
-
-    @pl.when(jnp.logical_not(fits))
+        for group in range(BLK // PART):
+            for chunk in range(group * count, (group + 1) * count):
+                product(chunk, (numbers[2, 0, chunk] // 8) * 8, 1)
+            after(group)
+
+    @pl.when(misfits != 0)
     def _():
-        @pl.loop(0, count)
-        def _(k):
-            chunk = group * count + k
-            begin = (numbers[2, 0, chunk] // 8) * 8
-            number = jnp.maximum(1, (numbers[2, 0, chunk + 1] - begin + WINDOW - 1) // WINDOW)
-
-            @pl.loop(0, number)
-            def _(step):
-                product(chunk, begin + step * WINDOW)
+        @pl.loop(0, BLK // PART)
+        def _(group):
+
+            @pl.loop(group * count, (group + 1) * count)
+            def _(chunk):
+                begin = (numbers[2, 0, chunk] // 8) * 8
+                steps = (numbers[2, 0, chunk + 1] - begin + WINDOW - 1) // WINDOW
+                product(chunk, begin, jnp.maximum(1, steps))
+
+            after(group)
 
 
 def gather(movie, footprint, entry_block, entry_owner, entry_slot):
@@ -214,8 +218,7 @@
             pltpu.VMEM((ENT, VOX), BF16),
             pltpu.VMEM((3, 8, 128), jnp.int32),
             pltpu.SMEM((3, 8, 128), jnp.int32),
-            pltpu.SemaphoreType.DMA((5,)),
-            pltpu.SemaphoreType.DMA((BLK // PART,)),
+            pltpu.SemaphoreType.DMA((6,)),
         ],
         compiler_params=pltpu.CompilerParams(vmem_limit_bytes=48 << 20),
         name="project",
@@ -233,7 +236,8 @@
 def pick(rows, sub):
     chosen = jnp.where(sub // 2 == 0, rows[0:1, :], rows[1:2, :])
     lane = iota((SUB, 128), 1) - lax.rem(sub, 2) * SUB
-    return jnp.sum(jnp.where(lane == iota((SUB, 128), 0), chosen, 0.0), axis=1, keepdims=True)
+    column = jnp.sum(jnp.where(lane == iota((SUB, 128), 0), chosen, 0.0), axis=1, keepdims=True)
+    return jnp.broadcast_to(column, (SUB, 128))
 
 
 def delayed(parts, steps):
@@ -376,6 +380,9 @@
     for section in range(4):
         if section:
             place(section)
+        if section >= 2:
+            for copy in started[(section - 2) * 7 : (section - 1) * 7]:
+                copy.wait_send()
         send_section(section)
 
     slots_iota = (iota((OWN, 128), 0) + 1).astype(F32)
@@ -454,13 +461,13 @@
     energy = parts[0, y, SUB : SUB + 2, :]
     for other_q in range(1, 4):
         energy = energy + parts[other_q, y, SUB : SUB + 2, :]
-    scale = pick(energy, y) + 1.0
+    scale = 1.0 / (pick(energy, y) + 1.0)
     target = []
     for frame in range(4):
         total = parts[0, frame, :SUB, :]
         for other_q in range(1, 4):
             total = total + parts[other_q, frame, :SUB, :]
-        target.append(total / scale)
+        target.append(total * scale)
     traced = sweeps(target, pick(slow[...], y), pick(fast[...], y))
     for frame in range(4):
         piece[frame] = traced[frame]
@@ -525,7 +532,7 @@
                     reply.at[0, pl.ds(0, CAP)], answer(index, section), s4.at[0], r4.at[index * 4 + section],
                     other(q),
                 ).wait_recv()
-    for copy in started:
+    for copy in started[14:]:
         if copy.is_remote:
             copy.wait_send()
         else:
@@ -578,12 +585,12 @@
                 pl.ds(numbers[0, line, lane], 1), :
             ]
 
-    def product(chunk, first):
+    def term(chunk, first):
         span = pl.ds(pl.multiple_of(first, 8), WINDOW)
         values, which = rows[span, :], block[span, :]
         masked = jnp.concatenate(
             [
-                jnp.where(which == (chunk * 8 + n).astype(F32), values, 0.0).astype(BF16)
+                jnp.where(which == jnp.asarray(chunk * 8 + n, F32), values, 0.0).astype(BF16)
                 for n in range(8)
             ],
             axis=1,
@@ -595,42 +602,20 @@
         span = pl.ds(number * PART, PART)
         return pltpu.make_async_copy(out.at[span], out_hbm.at[span], sem.at[number])
 
-    def store(chunk, result):
+    def product(chunk, begin, steps):
+        result = term(chunk, begin)
+        if not isinstance(steps, int):
+            total[...] = result
+
+            @pl.loop(1, steps)
+            def _(step):
+                total[...] += term(chunk, begin + step * WINDOW)
+
+            result = total[...]
         for n in range(8):
             out[chunk * 8 + n] = result[:, n * FR : (n + 1) * FR].astype(BF16)
 
-    count = PART // 8
-
-    @pl.loop(0, BLK // PART)
-    def _(group):
-        fits = None
-        for k in range(count):
-            chunk = group * count + k
-            inside = numbers[2, 0, chunk + 1] - (numbers[2, 0, chunk] // 8) * 8 <= WINDOW
-            fits = inside if fits is None else fits & inside
-
-        @pl.when(fits)
-        def _():
-            for k in range(count):
-                chunk = group * count + k
-                store(chunk, product(chunk, (numbers[2, 0, chunk] // 8) * 8))
-
-        @pl.when(jnp.logical_not(fits))
-        def _():
-            @pl.loop(0, count)
-            def _(k):
-                chunk = group * count + k
-                begin = (numbers[2, 0, chunk] // 8) * 8
-                number = jnp.maximum(1, (numbers[2, 0, chunk + 1] - begin + WINDOW - 1) // WINDOW)
-                total[...] = product(chunk, begin)
-
-                @pl.loop(1, number)
-                def _(step):
-                    total[...] += product(chunk, begin + step * WINDOW)
-
-                store(chunk, total[...])
-
-        out_part(group).start()
+    windows(numbers, product, lambda group: out_part(group).start())
 
     @pl.loop(0, BLK // PART)
     def _(group):

time: 61.5 us -> 59.3 us (0.964)
  Pallas kernels: 60 us -> 57.5 us
    pallas_call x1, Pallas kernels: 7 us -> 5.21 us  [gather(): pl.pallas_call(gather_kernel, out_shape=(shape((ENT + WINDOW, FR), F32),...]
where the time goes in v5:
time: 59.3 us; the launch traced here: 58.4 us
  Pallas kernels  57.5 us (97%)
  between operations  0.86 us (1%)
    pallas_call x1, Pallas kernels, exchange(): pl.pallas_call(exchange_kernel, out_shape=(jax.ShapeDtypeStruct((8 * ROWS...  45.3 us
    pallas_call x1, Pallas kernels, rebuild(): pl.pallas_call(rebuild_kernel, out_shape=(jax.ShapeDtypeStruct((BLK, VOX,...  7.06 us
    pallas_call x1, Pallas kernels, gather(): pl.pallas_call(gather_kernel, out_shape=(shape((ENT + WINDOW, FR), F32),...  5.21 us

profile of v5, /device:TPU:0, one launch (start us, length us, event | category | flops | bytes accessed | tf_op | source)
XLA Modules:
  0.0 58.4 jit_solution(10311441882544875486)
XLA Ops:
  0.6 0.0 copy-start.2
  0.6 0.0 copy-start.1
  0.7 0.0 copy-start
  0.7 5.2 %project.1 = (f32[1088,128]{1,0:T(8,128)S(1)}, f32[8,8,128]{2,1,0:T(8,128)S(1)}, s32[4,8,128]{2,1,0:T(8,128)S(1)}, s32[3,8,128]{2,1,0:T(8,128)S(1)}, f32[1088,128]{1,0:T(8,128)S(1)}, /*index=5*/f32[1088,128]{1,0:T(8,128)S(1)}) custom-call(bf16[256,128,128]{2,1,0:T(8,128)(2,1)} %movie_hbm.1, bf16[1024,128]{1,0:T(8,128)(2,1)} %foot_hbm.1, s32[8,128]{1,0:T(8,128)} %bitcast.7, ...), custom_call_target="tpu_custom_call" | custom-call | tf_op jit(solution)/shard_map/project/pallas_call | solution.py:204
  5.9 0.0 copy-done.2
  5.9 0.0 copy-done.1
  5.9 0.0 copy-done
  5.9 45.3 %exchange.1 = (f32[3136,128]{1,0:T(8,128)S(1)}, f32[256,128]{1,0:T(8,128)S(1)}) custom-call(f32[1088,128]{1,0:T(8,128)S(1)} %get-tuple-element.11.projected, f32[8,8,128]{2,1,0:T(8,128)S(1)} %get-tuple-element.12.labels, s32[4,8,128]{2,1,0:T(8,128)S(1)} %get-tuple-element.13.inverse_v, f32[256,128]{1,0:T(8,128)S(1)} %copy-done, f32[2,128]{1,0:T(2,128)S(1)} %bitcast.5, ...), custom_call_target="tpu_custom_call" | custom-call | tf_op jit(solution)/shard_map/exchange/pallas_call | solution.py:544
  51.2 7.1 %rebuild.1 = (bf16[256,128,128]{2,1,0:T(8,128)(2,1)}, f32[256,128]{1,0:T(8,128)}) custom-call(s32[3,8,128]{2,1,0:T(8,128)S(1)} %get-tuple-element.10.numbers_v, f32[3136,128]{1,0:T(8,128)S(1)} %get-tuple-element.14.back, f32[1088,128]{1,0:T(8,128)S(1)} %get-tuple-element.15.foot, f32[1088,128]{1,0:T(8,128)S(1)} %get-tuple-element.16.block, ...), custom_call_target="tpu_custom_call" | custom-call | tf_op jit(solution)/shard_map/rebuild/pallas_call | solution.py:626
Async XLA Ops:
  0.6 5.2 %copy-start.2 = (f32[256]{0:T(256)S(1)}, f32[256]{0:T(256)}, u32[]{:S(2)}) copy-start(f32[256]{0:T(256)} %param.15) | copy-start | bytes 3076
  0.6 5.2 %copy-start.1 = (f32[256]{0:T(256)S(1)}, f32[256]{0:T(256)}, u32[]{:S(2)}) copy-start(f32[256]{0:T(256)} %param.14) | copy-start | bytes 3076
  0.7 5.2 %copy-start = (f32[256,128]{1,0:T(8,128)S(1)}, f32[256,128]{1,0:T(8,128)}, u32[]{:S(2)}) copy-start(f32[256,128]{1,0:T(8,128)} %traces.1) | copy-start | bytes 393220

commit v6 on v5

--- a/solution.py
+++ b/solution.py
@@ -19,6 +19,7 @@
 PIECE = SUB + 8
 WINDOW = 64
 PART = 32
+STAGES = (352, 640, 896, 1024)
 MESH = pl.DeviceIdType.MESH
 F32 = jnp.float32
 BF16 = jnp.bfloat16
@@ -38,8 +39,8 @@
 
 def gather_kernel(
     movie_hbm, foot_hbm, block_hbm, owner_hbm, slot_hbm,
-    projected, labels, inverse, numbers, foot_sorted, block_sorted,
-    movie, foot, index, numbers_s, sem,
+    projected, labels, inverse, begins_out, places_out, foot_sorted, block_sorted,
+    movie, foot, index, begins_s, sem,
 ):
     small = [
         pltpu.make_async_copy(source, target, sem.at[number])
@@ -88,16 +89,16 @@
     tile, z = lax.axis_index("tile"), lax.axis_index("plane")
     turned = (member - jnp.where(core == 0, z, tile // 2) + 4) & 3
     section = jnp.where(turned == 0, 3, jnp.where(turned == 2, 0, jnp.where(turned == 1, 1, 2)))
-    numbers[0] = message * ROWS + 8 + section * CAP + rank
-    numbers[1] = order
+    pos = message * ROWS + 8 + section * CAP + rank
     begins = jnp.broadcast_to(jnp.sum(less, axis=0, keepdims=True), (8, 128)).astype(jnp.int32)
     beyond = pltpu.roll(begins, 127, 1) - (begins >> 3) * 8 > WINDOW
     lane = iota((8, 128), 1)
-    misfits = jnp.sum(
-        jnp.where(beyond & (lane < BLK // 8), 1.0, 0.0), axis=1, keepdims=True
-    ).astype(jnp.int32)
-    numbers[2] = jnp.where(lane == 127, misfits, begins)
-    to_smem = pltpu.make_async_copy(numbers, numbers_s, sem.at[4])
+    beyond = beyond & (lane < BLK // 8)
+    for chunk, rows in zip((7, 15, 23), STAGES):
+        beyond = beyond | ((lane == chunk) & ((begins >> 3) * 8 + WINDOW > rows))
+    misfits = jnp.sum(jnp.where(beyond, 1.0, 0.0), axis=1, keepdims=True).astype(jnp.int32)
+    begins_out[...] = jnp.where(lane == 127, misfits, begins)
+    to_smem = pltpu.make_async_copy(begins_out, begins_s, sem.at[4])
     to_smem.start()
 
     small[3].wait()
@@ -110,6 +111,7 @@
     place = section * 128 + rank
     meta = jnp.zeros((40, 512), F32)
     sorted_wide = jnp.zeros((ENT, 256), F32)
+    sorted_pos = jnp.zeros((16, ENT), F32)
     for row in range(8):
         lanes = slice(row * 128, row * 128 + 128)
         chosen = message[row : row + 1, :] == iota((8, 128), 0)
@@ -129,6 +131,13 @@
         places = jnp.where(place[row : row + 1, :] == iota((512, 128), 0), 1.0, 0.0).astype(BF16)
         meta += lax.dot_general(values, places, NT, preferred_element_type=F32)
         permute = jnp.where(order[row : row + 1, :] == iota((ENT, 128), 0), 1.0, 0.0).astype(BF16)
+        halves = [
+            jnp.broadcast_to(part[row : row + 1, :], (8, 128)).astype(F32)
+            for part in (pos >> 5, pos & 31)
+        ]
+        sorted_pos += lax.dot_general(
+            jnp.concatenate(halves, axis=0).astype(BF16), permute, NT, preferred_element_type=F32
+        )
         wide = jnp.concatenate(
             [
                 foot[lanes, :],
@@ -137,6 +146,9 @@
             axis=1,
         )
         sorted_wide += jnp.dot(permute, wide, preferred_element_type=F32)
+    sorted_pos = (sorted_pos[:8, :] * 32.0 + sorted_pos[8:, :]).astype(jnp.int32)
+    for row in range(8):
+        places_out[row : row + 1, :] = sorted_pos[:1, row * 128 : (row + 1) * 128]
     foot_sorted[:ENT, :] = sorted_wide[:, :128]
     block_sorted[:ENT, :] = sorted_wide[:, 128:]
     place_of = (meta[24:32, :] * 32.0 + meta[32:40, :]).astype(jnp.int32)
@@ -170,32 +182,38 @@
             pl.loop(0, steps)(add)
 
     load.wait()
-    windows(numbers_s, product, lambda group: None)
-
-
-def windows(numbers, product, after):
+    windows(begins_s, product)
+
+
+def windows(begins, product, ahead=None, after=None):
     count = PART // 8
-    misfits = numbers[2, 0, 127]
+    misfits = begins[0, 127]
 
     @pl.when(misfits == 0)
     def _():
         for group in range(BLK // PART):
+            if ahead is not None:
+                ahead(group)
             for chunk in range(group * count, (group + 1) * count):
-                product(chunk, (numbers[2, 0, chunk] // 8) * 8, 1)
-            after(group)
+                product(chunk, (begins[0, chunk] // 8) * 8, 1)
+            if after is not None:
+                after(group)
 
     @pl.when(misfits != 0)
     def _():
+        if ahead is not None:
+            ahead(None)
+
         @pl.loop(0, BLK // PART)
         def _(group):
-
             @pl.loop(group * count, (group + 1) * count)
             def _(chunk):
-                begin = (numbers[2, 0, chunk] // 8) * 8
-                steps = (numbers[2, 0, chunk + 1] - begin + WINDOW - 1) // WINDOW
+                begin = (begins[0, chunk] // 8) * 8
+                steps = (begins[0, chunk + 1] - begin + WINDOW - 1) // WINDOW
                 product(chunk, begin, jnp.maximum(1, steps))
 
-            after(group)
+            if after is not None:
+                after(group)
 
 
 def gather(movie, footprint, entry_block, entry_owner, entry_slot):
@@ -207,17 +225,18 @@
             shape((ENT + WINDOW, FR), F32),
             shape((8, 8, 128), F32),
             shape((4, 8, 128), jnp.int32),
-            shape((3, 8, 128), jnp.int32),
+            shape((8, 128), jnp.int32),
+            shape((8, 128), jnp.int32),
             shape((ENT + WINDOW, VOX), F32),
             shape((ENT + WINDOW, 128), F32),
         ),
         in_specs=[in_place] * 5,
-        out_specs=(VMEM,) * 6,
+        out_specs=(VMEM,) * 7,
         scratch_shapes=[
             pltpu.VMEM((BLK, VOX, FR), BF16),
             pltpu.VMEM((ENT, VOX), BF16),
             pltpu.VMEM((3, 8, 128), jnp.int32),
-            pltpu.SMEM((3, 8, 128), jnp.int32),
+            pltpu.SMEM((8, 128), jnp.int32),
             pltpu.SemaphoreType.DMA((6,)),
         ],
         compiler_params=pltpu.CompilerParams(vmem_limit_bytes=48 << 20),
@@ -570,20 +589,32 @@
 
 
 def rebuild_kernel(
-    numbers_v, back, foot, block, calcium, out_hbm, calcium_out, numbers, rows, out, total, sem
+    begins_v, places_v, back, foot, block, calcium, out_hbm, calcium_out,
+    begins, places, rows, out, total, sem,
 ):
-    to_smem = pltpu.make_async_copy(numbers_v, numbers, sem.at[BLK // PART])
-    to_smem.start()
+    to_smem = [
+        pltpu.make_async_copy(source, target, sem.at[BLK // PART + number])
+        for number, (source, target) in enumerate([(begins_v, begins), (places_v, places)])
+    ]
+    for copy in to_smem:
+        copy.start()
     calcium_out[...] = calcium[...]
     rows[ENT:, :] = jnp.zeros((WINDOW, FR), F32)
-    to_smem.wait()
-
-    @pl.loop(0, 8)
-    def _(line):
-        for lane in range(128):
-            rows[pl.ds(numbers[1, line, lane], 1), :] = back[
-                pl.ds(numbers[0, line, lane], 1), :
-            ]
+    for copy in to_smem:
+        copy.wait()
+
+    def stage(group):
+        if group is None:
+
+            @pl.loop(0, ENT // 128)
+            def _(line):
+                for lane in range(128):
+                    rows[pl.ds(line * 128 + lane, 1), :] = back[pl.ds(places[line, lane], 1), :]
+
+        elif group % 2 == 0:
+            number = group // 2
+            for row in range(STAGES[number - 1] if number else 0, STAGES[number]):
+                rows[row : row + 1, :] = back[pl.ds(places[row // 128, row % 128], 1), :]
 
     def term(chunk, first):
         span = pl.ds(pl.multiple_of(first, 8), WINDOW)
@@ -615,40 +646,41 @@
         for n in range(8):
             out[chunk * 8 + n] = result[:, n * FR : (n + 1) * FR].astype(BF16)
 
-    windows(numbers, product, lambda group: out_part(group).start())
+    windows(begins, product, stage, lambda group: out_part(group).start())
 
     @pl.loop(0, BLK // PART)
     def _(group):
         out_part(group).wait()
 
 
-def rebuild(numbers, back, foot, block, calcium):
+def rebuild(begins, places, back, foot, block, calcium):
     return pl.pallas_call(
         rebuild_kernel,
         out_shape=(
             jax.ShapeDtypeStruct((BLK, VOX, FR), BF16),
             jax.ShapeDtypeStruct((OWN, FR), F32),
         ),
-        in_specs=[VMEM] * 5,
+        in_specs=[VMEM] * 6,
         out_specs=(pl.BlockSpec(memory_space=pl.ANY), VMEM),
         scratch_shapes=[
-            pltpu.SMEM((3, 8, 128), jnp.int32),
+            pltpu.SMEM((8, 128), jnp.int32),
+            pltpu.SMEM((8, 128), jnp.int32),
             pltpu.VMEM((ENT + WINDOW, FR), F32),
             pltpu.VMEM((BLK, VOX, FR), BF16),
             pltpu.VMEM((VOX, 8 * FR), F32),
-            pltpu.SemaphoreType.DMA((BLK // PART + 1,)),
+            pltpu.SemaphoreType.DMA((BLK // PART + 2,)),
         ],
         compiler_params=pltpu.CompilerParams(vmem_limit_bytes=48 << 20),
         name="rebuild",
-    )(numbers, back, foot, block, calcium)
+    )(begins, places, back, foot, block, calcium)
 
 
 def shards(movie, footprint, entry_block, entry_owner, entry_slot, traces, slow_root, fast_root):
-    projected, labels, inverse, numbers, foot, block = gather(
+    projected, labels, inverse, begins, places, foot, block = gather(
         movie, footprint, entry_block, entry_owner, entry_slot
     )
     back, calcium = exchange(projected, labels, inverse, traces, slow_root, fast_root)
-    return rebuild(numbers, back, foot, block, calcium)
+    return rebuild(begins, places, back, foot, block, calcium)
 
 
 def solution(mesh):

time: 59.3 us -> 58.2 us (0.981)
  Pallas kernels: 57.5 us -> 56.5 us
    pallas_call x1, Pallas kernels: 7.06 us -> 5.5 us  [rebuild(): pl.pallas_call(rebuild_kernel, out_shape=(jax.ShapeDtypeStruct((BLK, VOX,...]
where the time goes in v6:
time: 58.2 us; the launch traced here: 57.4 us
  Pallas kernels  56.5 us (97%)
  between operations  0.86 us (1%)
    pallas_call x1, Pallas kernels, exchange(): pl.pallas_call(exchange_kernel, out_shape=(jax.ShapeDtypeStruct((8 * ROWS...  45.4 us
    pallas_call x1, Pallas kernels, gather(): pl.pallas_call(gather_kernel, out_shape=(shape((ENT + WINDOW, FR), F32),...  5.67 us
    pallas_call x1, Pallas kernels, rebuild(): pl.pallas_call(rebuild_kernel, out_shape=(jax.ShapeDtypeStruct((BLK, VOX,...  5.5 us

profile of v6, /device:TPU:0, one launch (start us, length us, event | category | flops | bytes accessed | tf_op | source)
XLA Modules:
  0.0 57.4 jit_solution(18187088608690164107)
XLA Ops:
  0.6 0.0 copy-start.2
  0.6 0.0 copy-start.1
  0.7 0.0 copy-start
  0.7 5.7 %project.1 = (f32[1088,128]{1,0:T(8,128)S(1)}, f32[8,8,128]{2,1,0:T(8,128)S(1)}, s32[4,8,128]{2,1,0:T(8,128)S(1)}, s32[8,128]{1,0:T(8,128)S(1)}, s32[8,128]{1,0:...) custom-call(bf16[256,128,128]{2,1,0:T(8,128)(2,1)} %movie_hbm.1, bf16[1024,128]{1,0:T(8,128)(2,1)} %foot_hbm.1, ...), custom_call_target="tpu_custom_call" | custom-call | tf_op jit(solution)/shard_map/project/pallas_call | solution.py:222
  6.3 0.0 copy-done.2
  6.4 0.0 copy-done.1
  6.4 0.0 copy-done
  6.4 45.4 %exchange.1 = (f32[3136,128]{1,0:T(8,128)S(1)}, f32[256,128]{1,0:T(8,128)S(1)}) custom-call(f32[1088,128]{1,0:T(8,128)S(1)} %get-tuple-element.13.projected, f32[8,8,128]{2,1,0:T(8,128)S(1)} %get-tuple-element.14.labels, s32[4,8,128]{2,1,0:T(8,128)S(1)} %get-tuple-element.15.inverse_v, f32[256,128]{1,0:T(8,128)S(1)} %copy-done, f32[2,128]{1,0:T(2,128)S(1)} %bitcast.5, ...), custom_call_target="tpu_custom_call" | custom-call | tf_op jit(solution)/shard_map/exchange/pallas_call | solution.py:563
  51.7 5.5 %rebuild.1 = (bf16[256,128,128]{2,1,0:T(8,128)(2,1)}, f32[256,128]{1,0:T(8,128)}) custom-call(s32[8,128]{1,0:T(8,128)S(1)} %get-tuple-element.11.begins_v, s32[8,128]{1,0:T(8,128)S(1)} %get-tuple-element.12.places_v, f32[3136,128]{1,0:T(8,128)S(1)} %get-tuple-element.16.back, f32[1088,128]{1,0:T(8,128)S(1)} %get-tuple-element.17.foot, ...), custom_call_target="tpu_custom_call" | custom-call | tf_op jit(solution)/shard_map/rebuild/pallas_call | solution.py:657
Async XLA Ops:
  0.6 5.7 %copy-start.2 = (f32[256]{0:T(256)S(1)}, f32[256]{0:T(256)}, u32[]{:S(2)}) copy-start(f32[256]{0:T(256)} %param.15) | copy-start | bytes 3076
  0.6 5.7 %copy-start.1 = (f32[256]{0:T(256)S(1)}, f32[256]{0:T(256)}, u32[]{:S(2)}) copy-start(f32[256]{0:T(256)} %param.14) | copy-start | bytes 3076
  0.7 5.7 %copy-start = (f32[256,128]{1,0:T(8,128)S(1)}, f32[256,128]{1,0:T(8,128)}, u32[]{:S(2)}) copy-start(f32[256,128]{1,0:T(8,128)} %traces.1) | copy-start | bytes 393220

commit v7 on v6

--- a/solution.py
+++ b/solution.py
@@ -39,7 +39,7 @@
 
 def gather_kernel(
     movie_hbm, foot_hbm, block_hbm, owner_hbm, slot_hbm,
-    projected, labels, inverse, begins_out, places_out, foot_sorted, block_sorted,
+    projected, codes, energies, begins_out, foot_sorted, block_sorted,
     movie, foot, index, begins_s, sem,
 ):
     small = [
@@ -108,36 +108,13 @@
     energy = lax.dot_general(ones, sq_high, NT, preferred_element_type=F32) + lax.dot_general(
         ones, sq_low, NT, preferred_element_type=F32
     )
-    place = section * 128 + rank
-    meta = jnp.zeros((40, 512), F32)
+    for number, code in enumerate((message, section * 128 + rank, order, pos, slt)):
+        codes[number] = code
+    energies[...] = energy
     sorted_wide = jnp.zeros((ENT, 256), F32)
-    sorted_pos = jnp.zeros((16, ENT), F32)
     for row in range(8):
         lanes = slice(row * 128, row * 128 + 128)
-        chosen = message[row : row + 1, :] == iota((8, 128), 0)
-        en_high, en_low = split(energy[:, lanes])
-        slots = (slt[row : row + 1, :] + 1).astype(F32)
-        sorted_at = order[row : row + 1, :] + 1
-        values = jnp.concatenate(
-            [
-                jnp.where(chosen, slots, 0.0),
-                jnp.where(chosen, en_high.astype(F32), 0.0),
-                jnp.where(chosen, en_low.astype(F32), 0.0),
-                jnp.where(chosen, (sorted_at >> 5).astype(F32), 0.0),
-                jnp.where(chosen, (sorted_at & 31).astype(F32), 0.0),
-            ],
-            axis=0,
-        ).astype(BF16)
-        places = jnp.where(place[row : row + 1, :] == iota((512, 128), 0), 1.0, 0.0).astype(BF16)
-        meta += lax.dot_general(values, places, NT, preferred_element_type=F32)
         permute = jnp.where(order[row : row + 1, :] == iota((ENT, 128), 0), 1.0, 0.0).astype(BF16)
-        halves = [
-            jnp.broadcast_to(part[row : row + 1, :], (8, 128)).astype(F32)
-            for part in (pos >> 5, pos & 31)
-        ]
-        sorted_pos += lax.dot_general(
-            jnp.concatenate(halves, axis=0).astype(BF16), permute, NT, preferred_element_type=F32
-        )
         wide = jnp.concatenate(
             [
                 foot[lanes, :],
@@ -146,19 +123,8 @@
             axis=1,
         )
         sorted_wide += jnp.dot(permute, wide, preferred_element_type=F32)
-    sorted_pos = (sorted_pos[:8, :] * 32.0 + sorted_pos[8:, :]).astype(jnp.int32)
-    for row in range(8):
-        places_out[row : row + 1, :] = sorted_pos[:1, row * 128 : (row + 1) * 128]
     foot_sorted[:ENT, :] = sorted_wide[:, :128]
     block_sorted[:ENT, :] = sorted_wide[:, 128:]
-    place_of = (meta[24:32, :] * 32.0 + meta[32:40, :]).astype(jnp.int32)
-    place_of = jnp.where(place_of == 0, ENT, place_of - 1)
-    weights = meta[8:16, :] + meta[16:24, :]
-    for i in range(4):
-        lanes = slice(i * 128, i * 128 + 128)
-        inverse[i] = place_of[:, lanes]
-        labels[:, i, :] = meta[:8, lanes]
-        labels[:, 4 + i, :] = weights[:, lanes]
     to_smem.wait()
 
     def product(chunk, begin, steps):
@@ -223,15 +189,14 @@
         gather_kernel,
         out_shape=(
             shape((ENT + WINDOW, FR), F32),
-            shape((8, 8, 128), F32),
-            shape((4, 8, 128), jnp.int32),
-            shape((8, 128), jnp.int32),
+            shape((5, 8, 128), jnp.int32),
+            shape((8, ENT), F32),
             shape((8, 128), jnp.int32),
             shape((ENT + WINDOW, VOX), F32),
             shape((ENT + WINDOW, 128), F32),
         ),
         in_specs=[in_place] * 5,
-        out_specs=(VMEM,) * 7,
+        out_specs=(VMEM,) * 6,
         scratch_shapes=[
             pltpu.VMEM((BLK, VOX, FR), BF16),
             pltpu.VMEM((ENT, VOX), BF16),
@@ -304,8 +269,8 @@
 
 
 def exchange_kernel(
-    projected, labels, inverse_v, traces, slow, fast, back, calcium,
-    inverse, send, got, hot, part, parts, piece, whole, reply,
+    projected, codes, energies, traces, slow, fast, back, calcium, places_out,
+    labels, inverse_v, inverse, send, got, hot, part, parts, piece, whole, reply,
     s1, r1, s2, r2, s3, r3, s4, r4, local,
 ):
     tile, y, z = lax.axis_index("tile"), lax.axis_index("tm"), lax.axis_index("plane")
@@ -326,8 +291,6 @@
     def column(pos, frame):
         return (d * 2 * x + c * (2 * pos + 1), frame, d * pos + c * z)
 
-    to_smem = pltpu.make_async_copy(inverse_v, inverse, local.at[0])
-    to_smem.start()
     reach = TURNS[:3]
     barrier = pltpu.get_barrier_semaphore()
     met = [mine(turn(p, by), c) for by in reach]
@@ -336,6 +299,32 @@
     met += [column(turn(q, dq), turn(y, dy)) for dq in TURNS for dy in TURNS if dq or dy]
     for device in met:
         pl.semaphore_signal(barrier, inc=1, device_id=device, device_id_type=MESH)
+    meta = jnp.zeros((40, 512), F32)
+    for row in range(8):
+        message_of, place_in, sorted_at, _, slots = [
+            codes[number, row : row + 1, :] for number in range(5)
+        ]
+        chosen = message_of == iota((8, 128), 0)
+        en_high, en_low = split(energies[:, row * 128 : row * 128 + 128])
+        sorted_at = sorted_at + 1
+        values = [
+            jnp.where(chosen, value.astype(F32), 0.0)
+            for value in (slots + 1, en_high, en_low, sorted_at >> 5, sorted_at & 31)
+        ]
+        spots = jnp.where(place_in == iota((512, 128), 0), 1.0, 0.0).astype(BF16)
+        meta += lax.dot_general(
+            jnp.concatenate(values, axis=0).astype(BF16), spots, NT, preferred_element_type=F32
+        )
+    place_of = (meta[24:32, :] * 32.0 + meta[32:40, :]).astype(jnp.int32)
+    place_of = jnp.where(place_of == 0, ENT, jnp.clip(place_of - 1, 0, ENT))
+    weights = meta[8:16, :] + meta[16:24, :]
+    for i in range(4):
+        lanes = slice(i * 128, i * 128 + 128)
+        inverse_v[i] = place_of[:, lanes]
+        labels[:, i, :] = meta[:8, lanes]
+        labels[:, 4 + i, :] = weights[:, lanes]
+    to_smem = pltpu.make_async_copy(inverse_v, inverse, local.at[0])
+    to_smem.start()
     for index in range(8):
         send[index * ROWS : index * ROWS + 8, :] = labels[index]
 
@@ -467,6 +456,19 @@
                         s2.at[section * 4 + dy], r2.at[q * 4 + y], column(tq, ty),
                     )
                 )
+    sorted_pos = jnp.zeros((16, ENT), F32)
+    for row in range(8):
+        sorted_at, pos = codes[2, row : row + 1, :], codes[3, row : row + 1, :]
+        permute = jnp.where(sorted_at == iota((ENT, 128), 0), 1.0, 0.0).astype(BF16)
+        halves = [
+            jnp.broadcast_to(part_of, (8, 128)).astype(F32) for part_of in (pos >> 5, pos & 31)
+        ]
+        sorted_pos += lax.dot_general(
+            jnp.concatenate(halves, axis=0).astype(BF16), permute, NT, preferred_element_type=F32
+        )
+    sorted_pos = (sorted_pos[:8, :] * 32.0 + sorted_pos[8:, :]).astype(jnp.int32)
+    for row in range(8):
+        places_out[row : row + 1, :] = sorted_pos[:1, row * 128 : (row + 1) * 128]
     own.wait()
     for dq in TURNS:
         for dy in TURNS:
@@ -558,17 +560,20 @@
             copy.wait()
 
 
-def exchange(projected, labels, inverse, traces, slow_root, fast_root):
+def exchange(projected, codes, energies, traces, slow_root, fast_root):
     dma = pltpu.SemaphoreType.DMA
     return pl.pallas_call(
         exchange_kernel,
         out_shape=(
             jax.ShapeDtypeStruct((8 * ROWS, FR), F32),
             jax.ShapeDtypeStruct((OWN, FR), F32),
+            jax.ShapeDtypeStruct((8, 128), jnp.int32),
         ),
         in_specs=[VMEM] * 6,
-        out_specs=(VMEM, VMEM),
+        out_specs=(VMEM, VMEM, VMEM),
         scratch_shapes=[
+            pltpu.VMEM((8, 8, 128), F32),
+            pltpu.VMEM((4, 8, 128), jnp.int32),
             pltpu.SMEM((4, 8, 128), jnp.int32),
             pltpu.VMEM((8 * ROWS, FR), F32),
             pltpu.VMEM((8, ROWS, FR), F32),
@@ -585,7 +590,7 @@
             collective_id=1, has_side_effects=True, vmem_limit_bytes=48 << 20
         ),
         name="exchange",
-    )(projected, labels, inverse, traces, slow_root.reshape(2, 128), fast_root.reshape(2, 128))
+    )(projected, codes, energies, traces, slow_root.reshape(2, 128), fast_root.reshape(2, 128))
 
 
 def rebuild_kernel(
@@ -676,10 +681,10 @@
 
 
 def shards(movie, footprint, entry_block, entry_owner, entry_slot, traces, slow_root, fast_root):
-    projected, labels, inverse, begins, places, foot, block = gather(
+    projected, codes, energies, begins, foot, block = gather(
         movie, footprint, entry_block, entry_owner, entry_slot
     )
-    back, calcium = exchange(projected, labels, inverse, traces, slow_root, fast_root)
+    back, calcium, places = exchange(projected, codes, energies, traces, slow_root, fast_root)
     return rebuild(begins, places, back, foot, block, calcium)
 
 

time: 58.2 us -> 57.7 us (level)
  no operation moved by 1% of the time
where the time goes in v7:
time: 57.7 us; the launch traced here: 57.4 us
  Pallas kernels  56.5 us (98%)
  between operations  0.86 us (1%)
    pallas_call x1, Pallas kernels, exchange(): pl.pallas_call(exchange_kernel, out_shape=(jax.ShapeDtypeStruct((8 * ROWS...  45.8 us
    pallas_call x1, Pallas kernels, rebuild(): pl.pallas_call(rebuild_kernel, out_shape=(jax.ShapeDtypeStruct((BLK, VOX,...  5.51 us
    pallas_call x1, Pallas kernels, gather(): pl.pallas_call(gather_kernel, out_shape=(shape((ENT + WINDOW, FR), F32),...  5.21 us

profile of v7, /device:TPU:0, one launch (start us, length us, event | category | flops | bytes accessed | tf_op | source)
XLA Modules:
  0.0 57.4 jit_solution(3032481805609159351)
XLA Ops:
  0.6 0.0 copy-start.2
  0.6 0.0 copy-start.1
  0.7 0.0 copy-start
  0.7 5.2 %project.1 = (f32[1088,128]{1,0:T(8,128)S(1)}, s32[5,8,128]{2,1,0:T(8,128)S(1)}, f32[8,1024]{1,0:T(8,128)S(1)}, s32[8,128]{1,0:T(8,128)S(1)}, f32[1088,128]{1,0:T(8,128)S(1)}, /*index=5*/f32[1088,128]{1,0:T(8,128)S(1)}) custom-call(bf16[256,128,128]{2,1,0:T(8,128)(2,1)} %movie_hbm.1, bf16[1024,128]{1,0:T(8,128)(2,1)} %foot_hbm.1, s32[8,128]{1,0:T(8,128)} %bitcast.7, ...), custom_call_target="tpu_custom_call" | custom-call | tf_op jit(solution)/shard_map/project/pallas_call | solution.py:188
  5.9 0.0 copy-done.2
  5.9 0.0 copy-done.1
  5.9 0.0 copy-done
  5.9 45.8 %exchange.1 = (f32[3136,128]{1,0:T(8,128)S(1)}, f32[256,128]{1,0:T(8,128)S(1)}, s32[8,128]{1,0:T(8,128)S(1)}) custom-call(f32[1088,128]{1,0:T(8,128)S(1)} %get-tuple-element.12.projected, s32[5,8,128]{2,1,0:T(8,128)S(1)} %get-tuple-element.13.codes, f32[8,1024]{1,0:T(8,128)S(1)} %get-tuple-element.14.energies, f32[256,128]{1,0:T(8,128)S(1)} %copy-done, ...), custom_call_target="tpu_custom_call" | custom-call | tf_op jit(solution)/shard_map/exchange/pallas_call | solution.py:565
  51.7 5.5 %rebuild.1 = (bf16[256,128,128]{2,1,0:T(8,128)(2,1)}, f32[256,128]{1,0:T(8,128)}) custom-call(s32[8,128]{1,0:T(8,128)S(1)} %get-tuple-element.11.begins_v, s32[8,128]{1,0:T(8,128)S(1)} %get-tuple-element.15.places_v, f32[3136,128]{1,0:T(8,128)S(1)} %get-tuple-element.16.back, f32[1088,128]{1,0:T(8,128)S(1)} %get-tuple-element.17.foot, ...), custom_call_target="tpu_custom_call" | custom-call | tf_op jit(solution)/shard_map/rebuild/pallas_call | solution.py:662
Async XLA Ops:
  0.6 5.2 %copy-start.2 = (f32[256]{0:T(256)S(1)}, f32[256]{0:T(256)}, u32[]{:S(2)}) copy-start(f32[256]{0:T(256)} %param.15) | copy-start | bytes 3076
  0.6 5.2 %copy-start.1 = (f32[256]{0:T(256)S(1)}, f32[256]{0:T(256)}, u32[]{:S(2)}) copy-start(f32[256]{0:T(256)} %param.14) | copy-start | bytes 3076
  0.7 5.2 %copy-start = (f32[256,128]{1,0:T(8,128)S(1)}, f32[256,128]{1,0:T(8,128)}, u32[]{:S(2)}) copy-start(f32[256,128]{1,0:T(8,128)} %traces.1) | copy-start | bytes 393220

commit v8 on v7

--- a/solution.py
+++ b/solution.py
@@ -7,6 +7,7 @@
 
 SWEEPS = 4
 TURNS = (2, 1, 3, 0)
+FAST_BLOCK = 32
 CAP = 96
 OWN = 256
 ENT = 1024
@@ -236,21 +237,61 @@
     return out
 
 
-def first_order(parts, powers):
-    for level, power in enumerate(powers):
-        moved = delayed(parts, 1 << level)
-        parts = [
-            part if late is None else part + power * late for part, late in zip(parts, moved)
-        ]
-    return parts
+def raised(root, count):
+    lane = iota(root.shape, 1)
+    value, power = jnp.ones_like(root), root
+    for level in range(count.bit_length() - 1):
+        value = jnp.where((lane >> level) & 1 == 1, value * power, value)
+        power = power * power
+    return value, power
+
+
+def running(count):
+    row, lane = iota((128, 128), 0), iota((128, 128), 1)
+    block = row // count == lane // count
+    sums = [jnp.where(block & (row <= lane), 1.0, 0.0), jnp.where(block, 1.0, 0.0)]
+    sums = jnp.concatenate(sums, axis=1).astype(BF16)
+    return jnp.concatenate([sums] * 3, axis=0)
+
+
+def first_order(parts, count, sums, value, inverse, power, root):
+    rows = parts[0].shape[0]
+    last = power / root
+    scaled = jnp.concatenate([part * inverse for part in parts], axis=0)
+    high = scaled.astype(BF16)
+    rest = scaled - high.astype(F32)
+    middle = rest.astype(BF16)
+    low = (rest - middle.astype(F32)).astype(BF16)
+    both = jnp.dot(
+        jnp.concatenate([high, middle, low], axis=1), sums, preferred_element_type=F32
+    )
+    cut = [both[index * rows : (index + 1) * rows] for index in range(len(parts))]
+    ends = [piece[:, 128:] * last for piece in cut]
+    if count == 128:
+        carry = [None, ends[0]]
+        for end in ends[1:-1]:
+            carry.append(end + power * carry[-1])
+    else:
+        carry, step = delayed(ends, count), count
+        while step < 512:
+            moved = delayed(carry, step)
+            carry = [
+                now if late is None else now + power * late for now, late in zip(carry, moved)
+            ]
+            step, power = 2 * step, power * power
+    after = value * root
+    return [
+        piece[:, :128] * value if late is None else piece[:, :128] * value + after * late
+        for piece, late in zip(cut, carry)
+    ]
 
 
 def sweeps(target, slow, fast):
     lag_one, lag_two = slow + fast, -slow * fast
-    slow_powers, fast_powers = [slow], [fast]
-    for _ in range(8):
-        slow_powers.append(slow_powers[-1] * slow_powers[-1])
-        fast_powers.append(fast_powers[-1] * fast_powers[-1])
+    settings = []
+    for root, count in ((slow, 128), (fast, FAST_BLOCK)):
+        value, power = raised(root, count)
+        settings.append((count, running(count), value, 1.0 / value, power, root))
     slow_share = slow / (slow - fast)
     fast_share = fast / (slow - fast)
     estimate = target
@@ -260,8 +301,8 @@
             jnp.maximum(now - lag_one * a - lag_two * b, 0.0)
             for now, a, b in zip(estimate, one, two)
         ]
-        slow_part = first_order(spikes, slow_powers)
-        fast_part = first_order(spikes, fast_powers)
+        slow_part = first_order(spikes, *settings[0])
+        fast_part = first_order(spikes, *settings[1])
         calcium = [slow_share * a - fast_share * b for a, b in zip(slow_part, fast_part)]
         if sweep + 1 < SWEEPS:
             estimate = [0.5 * (a + b) for a, b in zip(target, calcium)]

time: 57.7 us -> 57.5 us (level)
  no operation moved by 1% of the time
where the time goes in v8:
time: 57.5 us; the launch traced here: 57.2 us
  Pallas kernels  56.3 us (98%)
  between operations  0.86 us (1%)
    pallas_call x1, Pallas kernels, exchange(): pl.pallas_call(exchange_kernel, out_shape=(jax.ShapeDtypeStruct((8 * ROWS...  45.6 us
    pallas_call x1, Pallas kernels, rebuild(): pl.pallas_call(rebuild_kernel, out_shape=(jax.ShapeDtypeStruct((BLK, VOX,...  5.5 us
    pallas_call x1, Pallas kernels, gather(): pl.pallas_call(gather_kernel, out_shape=(shape((ENT + WINDOW, FR), F32),...  5.19 us

profile of v8, /device:TPU:0, one launch (start us, length us, event | category | flops | bytes accessed | tf_op | source)
XLA Modules:
  0.0 57.2 jit_solution(10539860632223777858)
XLA Ops:
  0.6 0.0 copy-start.2
  0.6 0.0 copy-start.1
  0.7 0.0 copy-start
  0.7 5.2 %project.1 = (f32[1088,128]{1,0:T(8,128)S(1)}, s32[5,8,128]{2,1,0:T(8,128)S(1)}, f32[8,1024]{1,0:T(8,128)S(1)}, s32[8,128]{1,0:T(8,128)S(1)}, f32[1088,128]{1,0:T(8,128)S(1)}, /*index=5*/f32[1088,128]{1,0:T(8,128)S(1)}) custom-call(bf16[256,128,128]{2,1,0:T(8,128)(2,1)} %movie_hbm.1, bf16[1024,128]{1,0:T(8,128)(2,1)} %foot_hbm.1, s32[8,128]{1,0:T(8,128)} %bitcast.7, ...), custom_call_target="tpu_custom_call" | custom-call | tf_op jit(solution)/shard_map/project/pallas_call | solution.py:189
  5.9 0.0 copy-done.2
  5.9 0.0 copy-done.1
  5.9 0.0 copy-done
  5.9 45.6 %exchange.1 = (f32[3136,128]{1,0:T(8,128)S(1)}, f32[256,128]{1,0:T(8,128)S(1)}, s32[8,128]{1,0:T(8,128)S(1)}) custom-call(f32[1088,128]{1,0:T(8,128)S(1)} %get-tuple-element.12.projected, s32[5,8,128]{2,1,0:T(8,128)S(1)} %get-tuple-element.13.codes, f32[8,1024]{1,0:T(8,128)S(1)} %get-tuple-element.14.energies, f32[256,128]{1,0:T(8,128)S(1)} %copy-done, ...), custom_call_target="tpu_custom_call" | custom-call | tf_op jit(solution)/shard_map/exchange/pallas_call | solution.py:606
  51.5 5.5 %rebuild.1 = (bf16[256,128,128]{2,1,0:T(8,128)(2,1)}, f32[256,128]{1,0:T(8,128)}) custom-call(s32[8,128]{1,0:T(8,128)S(1)} %get-tuple-element.11.begins_v, s32[8,128]{1,0:T(8,128)S(1)} %get-tuple-element.15.places_v, f32[3136,128]{1,0:T(8,128)S(1)} %get-tuple-element.16.back, f32[1088,128]{1,0:T(8,128)S(1)} %get-tuple-element.17.foot, ...), custom_call_target="tpu_custom_call" | custom-call | tf_op jit(solution)/shard_map/rebuild/pallas_call | solution.py:703
Async XLA Ops:
  0.6 5.2 %copy-start.2 = (f32[256]{0:T(256)S(1)}, f32[256]{0:T(256)}, u32[]{:S(2)}) copy-start(f32[256]{0:T(256)} %param.15) | copy-start | bytes 3076
  0.6 5.2 %copy-start.1 = (f32[256]{0:T(256)S(1)}, f32[256]{0:T(256)}, u32[]{:S(2)}) copy-start(f32[256]{0:T(256)} %param.14) | copy-start | bytes 3076
  0.7 5.2 %copy-start = (f32[256,128]{1,0:T(8,128)S(1)}, f32[256,128]{1,0:T(8,128)}, u32[]{:S(2)}) copy-start(f32[256,128]{1,0:T(8,128)} %traces.1) | copy-start | bytes 393220
